TPU v7x, 32 devices: a whole 2x2x4 slice. The times are simulated.
32 devices in a mesh: wide: 16 (over z, y, x), narrow: 2 (over core).
Axes of the slice: x: 2, y: 2, z: 4, core: 2. Of those that a mesh axis runs over, the one named last changes fastest.
Arguments:
- incoming_activations: bfloat16 [32768, 768], P(('wide', 'narrow')), may hold values from -6 to 6
- span_identifiers: int32 [64, 512], P(('wide', 'narrow')), may hold values from 0 to 7, never falling along the last dimension, each value on 1 to 128 neighbouring positions
- partner_global_index: int32 [512], replicated, may hold values from 0 to 511, as said below
- softmax_coolness: float32 [1], replicated, may hold values from 0.03 to 0.06
- triple_kernel_panel: bfloat16 [768, 2304], replicated, may hold values from -0.21875 to 0.21875
- asking_shift: float32 [768], replicated, may hold values from -0.6 to 0.6
- content_shift: float32 [768], replicated, may hold values from -0.6 to 0.6
- mixer_result_kernel: bfloat16 [768, 768], replicated, may hold values from -1.75 to 1.75
- mixer_result_shift: float32 [768], replicated, may hold values from -0.6 to 0.6
- initial_standardize_scale: float32 [768], replicated, may hold values from 0.5 to 1.5
- initial_standardize_shift: float32 [768], replicated, may hold values from -0.6 to 0.6
- perceptron_entry_kernel: bfloat16 [768, 3072], replicated, may hold values from -0.21875 to 0.21875
- perceptron_entry_shift: float32 [3072], replicated, may hold values from -0.6 to 0.6
- perceptron_result_kernel: bfloat16 [3072, 768], replicated, may hold values from -0.109375 to 0.109375
- perceptron_result_shift: float32 [768], replicated, may hold values from -0.6 to 0.6
- later_standardize_scale: float32 [768], replicated, may hold values from 0.5 to 1.5
- later_standardize_shift: float32 [768], replicated, may hold values from -0.6 to 0.6
Outputs:
- loss: float32 [1], replicated
- layer_out: bfloat16 [32768, 768], P(('wide', 'narrow'))
- input_grad: float32 [32768, 768], P(('wide', 'narrow'))
- attn_weight_grad: float32 [768, 2304], replicated
- query_bias_grad: float32 [768], replicated
- value_bias_grad: float32 [768], replicated
- merge_weight_grad: float32 [768, 768], replicated
- merge_bias_grad: float32 [768], replicated
- first_gain_grad: float32 [768], replicated
- first_shift_grad: float32 [768], replicated
- inner_weight_grad: float32 [768, 3072], replicated
- inner_bias_grad: float32 [3072], replicated
- outer_weight_grad: float32 [3072, 768], replicated
- outer_bias_grad: float32 [768], replicated
- second_gain_grad: float32 [768], replicated
- second_shift_grad: float32 [768], replicated
Inputs may be any that keep to these rules, and one draw needn't show every extreme that they name: `span_identifiers`: in each packed row the segment numbers never fall and every number below 8 occurs, none on more than 128 tokens. `partner_global_index`: a permutation of the segments with no segment its own partner.
All inputs are finite; a program needn't handle non-finite values.
Results may differ from a plain program's by a relative error of at most 0.008.
Values may be sent and summed in bfloat16 or wider, within the bound.
No kernel may reach another device: no remote copies, remote signals or barrier semaphores. Data moves between devices by JAX's collectives and lax.ppermute only.
A program may use at most 192 MiB of HBM per device.

v0:
```python
from functools import partial

import jax
import jax.numpy as jnp
from jax import lax
from jax.sharding import PartitionSpec as P

HEADS = 12
S_ROW = 8


HIGHEST = lax.Precision.HIGHEST


def joined(value, axis, join):
    pieces = jax.tree.map(lambda part: lax.all_gather(part, axis), value)
    head = jax.tree.map(lambda part: part[0], pieces)
    tail = jax.tree.map(lambda part: part[1:], pieces)
    total, _ = lax.scan(lambda total, section: (join(total, section), None), head, tail)
    return total


def layer_norm(values, gain, shift):
    center = values - jnp.mean(values, axis=-1, keepdims=True)
    spread = jnp.mean(center * center, axis=-1, keepdims=True)
    return center * lax.rsqrt(spread + 1e-05) * gain + shift


def left_dot(left, right):
    return lax.dot_general(
        left, right, (((0,), (0,)), ((), ())), preferred_element_type=jnp.float32
    )


def right_dot(left, right):
    return lax.dot_general(
        left, right, (((1,), (1,)), ((), ())), preferred_element_type=jnp.float32
    )


def row_scores(packed, segment_row):
    length = packed.shape[0]
    width = packed.shape[1] // 3
    head_size = width // HEADS
    split = packed.reshape(length, 3, HEADS, head_size)
    raw = jnp.einsum(
        "qhd,khd->hqk", split[:, 0], split[:, 1], preferred_element_type=jnp.float32
    ) * head_size ** (-0.5)
    same = segment_row[:, None] == segment_row[None, :]
    return (split, jnp.where(same[None], raw, -1000000000.0))


def attend_row(pair):
    packed, segment_row = pair
    split, masked = row_scores(packed, segment_row)
    top = jnp.max(masked, axis=-1, keepdims=True)
    exps = jnp.exp(masked - top)
    summed = jnp.sum(exps, axis=-1, keepdims=True)
    probs = exps / summed
    mixed = jnp.einsum(
        "hqk,khd->qhd", probs.astype(jnp.bfloat16), split[:, 2], preferred_element_type=jnp.float32
    )
    return (mixed.reshape(packed.shape[0], -1).astype(jnp.bfloat16), top + jnp.log(summed))


def attend_back(group):
    packed, segment_row, log_total, grad_mixed = group
    length = packed.shape[0]
    width = packed.shape[1] // 3
    head_size = width // HEADS
    split, masked = row_scores(packed, segment_row)
    probs = jnp.exp(masked - log_total)
    grad_split = grad_mixed.reshape(length, HEADS, head_size)
    grad_probs = jnp.einsum(
        "qhd,khd->hqk", grad_split, split[:, 2], preferred_element_type=jnp.float32
    )
    grad_values = jnp.einsum(
        "hqk,qhd->khd", probs.astype(jnp.bfloat16), grad_split, preferred_element_type=jnp.float32
    )
    inner_sum = jnp.sum(probs * grad_probs, axis=-1, keepdims=True)
    grad_raw = (probs * (grad_probs - inner_sum)).astype(jnp.bfloat16)
    scale = head_size ** (-0.5)
    grad_queries = (
        jnp.einsum("hqk,khd->qhd", grad_raw, split[:, 1], preferred_element_type=jnp.float32)
        * scale
    )
    grad_keys = (
        jnp.einsum("hqk,qhd->khd", grad_raw, split[:, 0], preferred_element_type=jnp.float32)
        * scale
    )
    stacked = jnp.stack([grad_queries, grad_keys, grad_values], axis=1)
    return stacked.reshape(length, 3 * width).astype(jnp.bfloat16)


def tile_logits(source_vector_code, target_vector_code, softmax_coolness, self_pair_filter):
    width_all = source_vector_code.shape[1]
    stacks = []
    for factor in (12, 8, 4, 2, 1):
        width = width_all * factor // 12
        row_part = source_vector_code[:, :width]
        col_part = target_vector_code[:, :width]
        row_unit = row_part * lax.rsqrt(jnp.sum(row_part * row_part, axis=1, keepdims=True) + 1e-06)
        col_unit = col_part * lax.rsqrt(jnp.sum(col_part * col_part, axis=1, keepdims=True) + 1e-06)
        cosine_logits = (
            lax.dot_general(
                row_unit,
                col_unit,
                (((1,), (1,)), ((), ())),
                precision=HIGHEST,
                preferred_element_type=jnp.float32,
            )
            / softmax_coolness[0]
        )
        stacks.append(jnp.where(self_pair_filter, -1000000000.0, cosine_logits))
    return jnp.stack(stacks)


def combine_stats(first, second):
    top = jnp.maximum(first[0], second[0])
    summed = first[1] * jnp.exp(first[0] - top) + second[1] * jnp.exp(second[0] - top)
    return (top, summed, first[2] + second[2])


def on_device(
    incoming_activations,
    span_identifiers,
    partner_global_index,
    softmax_coolness,
    triple_kernel_panel,
    asking_shift,
    content_shift,
    mixer_result_kernel,
    mixer_result_shift,
    initial_standardize_scale,
    initial_standardize_shift,
    perceptron_entry_kernel,
    perceptron_entry_shift,
    perceptron_result_kernel,
    perceptron_result_shift,
    later_standardize_scale,
    later_standardize_shift,
):
    row_count, length = span_identifiers.shape
    width = incoming_activations.shape[1]
    seg_dev = row_count * S_ROW
    inputs = incoming_activations.astype(jnp.float32)
    zero_bias = jnp.zeros_like(asking_shift)
    projected = (
        jnp.dot(incoming_activations, triple_kernel_panel, preferred_element_type=jnp.float32)
        + jnp.concatenate([asking_shift, zero_bias, content_shift])
    ).astype(jnp.bfloat16)
    packed_rows = projected.reshape(row_count, length, 3 * width)
    mixed_rows, log_totals = lax.map(attend_row, (packed_rows, span_identifiers))
    mixed = mixed_rows.reshape(row_count * length, width)
    attn = (
        jnp.dot(mixed, mixer_result_kernel, preferred_element_type=jnp.float32) + mixer_result_shift
    )
    normed, first_back = jax.vjp(
        layer_norm, inputs + attn, initial_standardize_scale, initial_standardize_shift
    )
    normed_low = normed.astype(jnp.bfloat16)
    inner = (
        jnp.dot(normed_low, perceptron_entry_kernel, preferred_element_type=jnp.float32)
        + perceptron_entry_shift
    )
    active_full, gelu_back = jax.vjp(partial(jax.nn.gelu, approximate=False), inner)
    active = active_full.astype(jnp.bfloat16)
    outer = (
        jnp.dot(active, perceptron_result_kernel, preferred_element_type=jnp.float32)
        + perceptron_result_shift
    )
    output, second_back = jax.vjp(
        layer_norm, normed + outer, later_standardize_scale, later_standardize_shift
    )
    layer_out = output.astype(jnp.bfloat16)
    onehot = (span_identifiers[:, :, None] == jnp.arange(S_ROW)[None, None, :]).astype(jnp.float32)
    counts = jnp.sum(onehot, axis=1)
    pooled = (
        jnp.einsum(
            "rls,rld->rsd", onehot, output.reshape(row_count, length, width), precision=HIGHEST
        )
        / counts[..., None]
    )
    span_pooled_code = pooled.reshape(seg_dev, width).astype(jnp.bfloat16)
    wide_index = lax.axis_index("wide")
    narrow_index = lax.axis_index("narrow")
    wide_size = lax.axis_size("wide")
    narrow_size = lax.axis_size("narrow")
    source_vector_code = lax.all_gather(span_pooled_code, "narrow", axis=0, tiled=True)
    target_vector_code = lax.all_gather(span_pooled_code, "wide", axis=0, tiled=True)
    tile_rows = narrow_size * seg_dev
    row_ids = wide_index * tile_rows + jnp.arange(tile_rows, dtype=jnp.int32)
    col_local = jnp.arange(wide_size * seg_dev, dtype=jnp.int32)
    col_ids = (col_local // seg_dev * narrow_size + narrow_index) * seg_dev + col_local % seg_dev
    row_positive = lax.dynamic_slice_in_dim(partner_global_index, wide_index * tile_rows, tile_rows)
    self_pair_filter = row_ids[:, None] == col_ids[None, :]
    hit_mask = row_positive[:, None] == col_ids[None, :]
    cosine_logits, tile_back = jax.vjp(
        partial(tile_logits, softmax_coolness=softmax_coolness, self_pair_filter=self_pair_filter),
        source_vector_code.astype(jnp.float32),
        target_vector_code.astype(jnp.float32),
    )
    top = jnp.max(cosine_logits, axis=2)
    summed = jnp.sum(jnp.exp(cosine_logits - top[..., None]), axis=2)
    hits = jnp.sum(jnp.where(hit_mask[None], cosine_logits, 0.0), axis=2)
    top, summed, hits = joined((top, summed, hits), "narrow", combine_stats)
    log_total = top + jnp.log(summed)
    loss = lax.psum(jnp.sum(log_total - hits), "wide")
    grad_scores = jnp.exp(cosine_logits - log_total[..., None]) - hit_mask[None].astype(jnp.float32)
    grad_row, grad_col = tile_back(grad_scores)
    grad_embed = lax.psum_scatter(
        grad_row, "narrow", scatter_dimension=0, tiled=True
    ) + lax.psum_scatter(grad_col, "wide", scatter_dimension=0, tiled=True)
    per_segment = grad_embed.reshape(row_count, S_ROW, width) / counts[..., None]
    grad_output = jnp.einsum("rls,rsd->rld", onehot, per_segment, precision=HIGHEST).reshape(
        row_count * length, width
    )
    grad_second, grad_second_gain, grad_second_shift = second_back(grad_output)
    grad_outer = grad_second.astype(jnp.bfloat16)
    grad_outer_weight = left_dot(active, grad_outer)
    grad_outer_bias = jnp.sum(grad_outer.astype(jnp.float32), axis=0)
    grad_active = right_dot(grad_outer, perceptron_result_kernel)
    grad_inner = gelu_back(grad_active)[0].astype(jnp.bfloat16)
    grad_inner_weight = left_dot(normed_low, grad_inner)
    grad_inner_bias = jnp.sum(grad_inner.astype(jnp.float32), axis=0)
    grad_normed = grad_second + right_dot(grad_inner, perceptron_entry_kernel)
    (
        grad_inner_weight,
        grad_inner_bias,
        grad_outer_weight,
        grad_outer_bias,
        grad_second_gain,
        grad_second_shift,
    ) = lax.psum(
        (
            grad_inner_weight,
            grad_inner_bias,
            grad_outer_weight,
            grad_outer_bias,
            grad_second_gain,
            grad_second_shift,
        ),
        ("wide", "narrow"),
    )
    grad_first, grad_first_gain, grad_first_shift = first_back(grad_normed)
    grad_attn = grad_first.astype(jnp.bfloat16)
    grad_merge_weight = left_dot(mixed, grad_attn)
    grad_merge_bias = jnp.sum(grad_attn.astype(jnp.float32), axis=0)
    grad_mixed = right_dot(grad_attn, mixer_result_kernel).astype(jnp.bfloat16)
    grad_packed = lax.map(
        attend_back,
        (packed_rows, span_identifiers, log_totals, grad_mixed.reshape(row_count, length, width)),
    )
    grad_packed = grad_packed.reshape(row_count * length, 3 * width)
    grad_attn_weight = left_dot(incoming_activations, grad_packed)
    bias_sums = jnp.sum(grad_packed.astype(jnp.float32), axis=0)
    grad_query_bias = bias_sums[:width]
    grad_value_bias = bias_sums[2 * width :]
    input_grad = grad_first + right_dot(grad_packed, triple_kernel_panel)
    (
        grad_attn_weight,
        grad_query_bias,
        grad_value_bias,
        grad_merge_weight,
        grad_merge_bias,
        grad_first_gain,
        grad_first_shift,
    ) = lax.psum(
        (
            grad_attn_weight,
            grad_query_bias,
            grad_value_bias,
            grad_merge_weight,
            grad_merge_bias,
            grad_first_gain,
            grad_first_shift,
        ),
        ("wide", "narrow"),
    )
    return (
        loss.reshape(1),
        layer_out,
        input_grad,
        grad_attn_weight,
        grad_query_bias,
        grad_value_bias,
        grad_merge_weight,
        grad_merge_bias,
        grad_first_gain,
        grad_first_shift,
        grad_inner_weight,
        grad_inner_bias,
        grad_outer_weight,
        grad_outer_bias,
        grad_second_gain,
        grad_second_shift,
    )


def solution(mesh):
    return jax.shard_map(
        on_device,
        mesh=mesh,
        in_specs=(
            P(("wide", "narrow"), None),
            P(("wide", "narrow"), None),
            P(),
            P(),
            P(),
            P(),
            P(),
            P(),
            P(),
            P(),
            P(),
            P(),
            P(),
            P(),
            P(),
            P(),
            P(),
        ),
        out_specs=(
            P(),
            P(("wide", "narrow"), None),
            P(("wide", "narrow"), None),
            P(),
            P(),
            P(),
            P(),
            P(),
            P(),
            P(),
            P(),
            P(),
            P(),
            P(),
            P(),
            P(),
        ),
        check_vma=False,
    )
```

profile of v0, /device:TPU:0, one launch (start us, length us, event | category | flops | bytes accessed | tf_op | source)
XLA Modules:
  0.0 964.9 jit_solution(957077554124767410)
XLA Ops:
  10.1 7.3 add_convert_fusion.1
  17.4 6.7 copy.67
  24.1 36.8 %while.7 = (s32[]{:T(128)}, bf16[2,512,768]{2,1,0:T(8,128)(2,1)}, f32[2,12,512,1]{2,1,3,0:T(8,128)}, bf16[2,512,2304]{1,2,0:T(8,128)(2,1)}, s32[2,512]{1,0:T(2,128)S(1)}, /*index=5*/s32[]{:T(128)}) while((s32[]{:T(128)}, bf16[2,512,768]{2,1,0:T(8,128)(2,1)}, f32[2,12,512,1]{2,1,3,0:T(8,128)}, bf16[2,512,2304]{1,2,0:T(8,128)(2,1)}, ...), condition=%wide.region_3.4_spmd, body=%wide.region_0.3_spmd.sunk | while | flops 843704320 | bytes 60913868 | solution.py:153
  24.3 1.9 constant_dynamic-slice_fusion.11
  26.3 2.1 fusion.202
  28.4 3.5 fusion.203
  32.0 5.5 fusion.204
  38.1 2.3 copy.91
  40.4 2.1 constant_dynamic-update-slice_fusion.4
  42.7 1.9 constant_dynamic-slice_fusion.11
  44.6 2.1 fusion.202
  46.8 3.5 fusion.203
  50.3 5.5 fusion.204
  56.5 2.3 copy.91
  58.8 2.1 constant_dynamic-update-slice_fusion.4
  60.9 3.9 fusion.158
  66.5 37.6 %multiply_convert_fusion.3 = (bf16[1024,3072]{1,0:T(8,128)(2,1)S(1)}, f32[1024,3072]{1,0:T(8,128)}, f32[1024,3072]{1,0:T(8,128)}) fusion(f32[3072]{0:T(1024)S(1)} %copy-done.49, bf16[768,3072]{1,0:T(8,128)(2,1)} %param.32, f32[1024,768]{1,0:T(8,128)S(1)} %get-tuple-element.246, f32[768]{0:T(1024)S(1)} %copy-done.30, f32[768]{0:T(1024)S(1)} %copy-done.26, ...), kind=kOutput, calls=%fused_computation.48 | convolution fusion | flops 5043388416 | bytes 39348224 | tf_op jit(solution)/shard_map/dot_general | solution.py:163
  104.2 5.4 fusion.159
  113.1 1.9 all_gather.24
  118.5 44.5 %all_gather.25 = bf16[256,768]{1,0:T(8,128)(2,1)S(1)} all-gather(bf16[16,768]{1,0:T(8,128)(2,1)S(1)} %fusion.47), channel_id=1, replica_groups=mesh['wide'=16,'narrow'=2] {'wide'}, dimensions={0}, use_global_device_ids=true | all-gather | bytes 417792 | tf_op jit(solution)/shard_map/all_gather | solution.py:190
  182.1 2.5 fusion.40
  184.6 2.3 fusion.46
  187.0 2.0 fusion.43
  189.0 1.9 fusion.37
  190.8 1.8 fusion.34
  199.0 1.9 all-gather.3
  225.8 1.9 multiply_reduce_fusion.8
  228.4 2.1 multiply_reduce_fusion.6
  235.7 118.3 %reduce-scatter.5.cloned.1.call-done = f32[16,768]{1,0:T(8,128)} async-done(((f32[256,768]{1,0:T(8,128)}), f32[16,768]{1,0:T(8,128)}) %reduce-scatter.5.cloned.1.call-update) | async-done | bytes 49168 | tf_op jit(solution)/shard_map/reduce_scatter | solution.py:213
  354.1 3.0 fusion.160
  357.1 2.3 fusion.29
  361.0 2.3 convert_reduce_fusion.2
  363.4 18.9 %convert_reduce_fusion = (f32[3072]{0:T(1024)}, bf16[1024,3072]{1,0:T(8,128)(2,1)}) fusion(f32[1024,3072]{1,0:T(8,128)} %get-tuple-element.236, bf16[1024,768]{1,0:T(8,128)(2,1)} %get-tuple-element.224, bf16[3072,768]{1,0:T(8,128)(2,1)} %param.34, f32[1024,3072]{1,0:T(8,128)} %get-tuple-element.247, f32[3072]{0:T(1024)S(1)} %copy-done.50), kind=kOutput, calls=%fused_computation.46 | convolution fusion | flops 4885312512 | bytes 37773312 | tf_op jit(solution)/shard_map/dot_general | solution.py:36
  382.3 10.8 %multiply_reduce_fusion.1 = (f32[768]{0:T(1024)}, f32[1024]{0:T(1024)S(1)}, f32[768]{0:T(1024)}, f32[1024,768]{1,0:T(8,128)S(1)}) fusion(f32[1024,768]{1,0:T(8,128)S(1)} %copy-done.12, f32[1024]{0:T(1024)S(1)} %fusion.129, f32[1024]{0:T(1024)S(1)} %broadcast_multiply_fusion.1, f32[768]{0:T(1024)S(1)} %copy-done.27, ...), kind=kOutput, calls=%fused_computation.71 | convolution fusion | flops 4839699456 | bytes 20472832 | tf_op jit(solution)/shard_map/dot_general | solution.py:36
  393.0 8.5 fusion.148
  405.8 2.9 fusion.161
  408.7 2.6 convolution_convert_fusion
  411.3 7.7 fusion.162
  419.0 65.6 %while.8 = (s32[]{:T(128)}, bf16[2,512,2304]{1,2,0:T(8,128)(2,1)}, bf16[2,512,2304]{1,2,0:T(8,128)(2,1)}, s32[2,512]{1,0:T(2,128)S(1)}, f32[2,12,512,1]{2,1,3,0:...) while((s32[]{:T(128)}, bf16[2,512,2304]{1,2,0:T(8,128)(2,1)}, bf16[2,512,2304]{1,2,0:T(8,128)(2,1)}, ...), condition=%wide.region_42.43_spmd, body=%wide.region_40.42_spmd.sunk | while | flops 2065033216 | bytes 143939856 | solution.py:250
  421.3 2.1 constant_dynamic-slice_fusion.12
  423.4 2.3 copy.92
  427.5 1.8 fusion.210
  429.4 3.1 fusion.211
  432.6 7.2 multiply_reduce_fusion.27
  439.7 7.1 multiply_convert_fusion.5
  448.0 2.0 fusion.212
  454.1 2.1 constant_dynamic-slice_fusion.12
  456.1 2.3 copy.92
  460.3 1.8 fusion.210
  462.2 3.1 fusion.211
  465.3 7.2 multiply_reduce_fusion.27
  472.5 7.1 multiply_convert_fusion.5
  480.8 2.0 fusion.212
  484.6 6.9 copy.77
  491.5 9.7 %convolution_bitcast_fusion = f32[768,2304]{0,1:T(8,128)} fusion(bf16[1024,2304]{1,0:T(8,128)(2,1)} %bitcast.288, bf16[1024,768]{1,0:T(8,128)(2,1)} %param.21), kind=kOutput, calls=%fused_computation.64 | convolution fusion | flops 3623878656 | bytes 13369344 | tf_op jit(solution)/shard_map/dot_general | solution.py:30
  501.3 42.1 %psum.98 = f32[1]{0:T(128)} all-reduce(f32[1]{0:T(128)} %bitcast.40), channel_id=1, replica_groups=mesh['wide'=16,'narrow'=2] {'wide'}, use_global_device_ids=true, to_apply=%region_23.24 | all-reduce | flops 1 | bytes 8 | tf_op jit(solution)/shard_map/psum | solution.py:208
  543.4 3.2 convert_reduce_fusion.1
  547.2 40.4 %all-reduce.8 = (f32[768]{0:T(1024)}, f32[768]{0:T(1024)}, f32[768]{0:T(1024)}, f32[768]{0:T(1024)}, f32[768]{0:T(1024)}, /*index=5*/f32[3072]{0:T(1024)}, f32[768]{0:T(1024)}, f32[768]{0:T(1024)}, f32[768]{0:T(1024)}) all-reduce(f32[768]{0:T(1024)} %get-tuple-element.242, ...), channel_id=1, replica_groups=mesh['wide'=16,'narrow'=2] {'wide','narrow'}, use_global_device_ids=true, to_apply=%region_45.46 | all-reduce | flops 9216 | bytes 73728 | tf_op jit(solution)/shard_map/psum | solution.py:268
  587.6 8.3 add_add_fusion.4
  595.9 338.4 %all-reduce.12.cloned.1.call-done = (f32[768,2304]{0,1:T(8,128)}, f32[768,768]{1,0:T(8,128)}, f32[768,3072]{1,0:T(8,128)}, f32[3072,768]{1,0:T(8,128)}) async-done(((f32[768,2304]{0,1:T(8,128)}, f32[768,768]{1,0:T(8,128)}, f32[768,3072]{1,0:T(8,128)}, f32[3072,768]{1,0:T(8,128)}), (f32[768,2304]{0,1:T(8,128)}, f32[768,768]{1,0:T(8,128)}, f32[768,3072]{1,0:T(8,128)}, ...) | async-done | bytes 28311568 | tf_op jit(solution)/shard_map/psum | solution.py:268
  934.3 8.0 copy.78
  942.2 3.4 copy.122
  945.6 8.8 copy.123
  954.4 3.7 copy.124
  (252 shorter events, 89.3 us)
Async XLA Ops:
  7.2 3.0 copy-start
  7.2 228.5 %reduce-scatter.3.cloned.1.call-start = ((), (), s32[]{:S(2)}) async-start(), calls=%async_computation.2 | async-start | bytes 147456 | tf_op jit(solution)/shard_map/reduce_scatter | solution.py:211
  17.4 6.7 copy-start.25
  24.1 36.8 %copy-start.51 = (f32[768]{0:T(1024)S(1)}, f32[768]{0:T(1024)}, u32[]{:S(2)}) copy-start(f32[768]{0:T(1024)} %param.29) | copy-start | bytes 9220
  24.3 4.1 copy-start.6
  26.3 2.2 copy-start.3
  31.9 5.5 copy-start.23
  42.7 4.1 copy-start.6
  44.6 2.2 copy-start.3
  50.3 5.5 copy-start.23
  60.9 5.5 copy-start.26
  60.9 5.5 copy-start.30
  60.9 5.5 copy-start.49
  60.9 43.2 %slice-start.3 = ((s8[4718592]{0:T(1024)(128)(4,1)}), s8[4194304]{0:T(1024)(128)(4,1)S(1)}, s32[]{:S(2)}) async-start(s8[4718592]{0:T(1024)(128)(4,1)} %bitcast.296), calls=%async_computation.8 | async-start | bytes 8388608
  64.9 39.2 %copy-start.11 = (f32[1024,768]{1,0:T(8,128)}, f32[1024,768]{1,0:T(8,128)S(1)}, u32[]{:S(2)}) copy-start(f32[1024,768]{1,0:T(8,128)S(1)} %get-tuple-element.246) | copy-start | bytes 9437188
  66.4 37.7 %slice-start.4 = ((s8[4718592]{0:T(1024)(128)(4,1)}), s8[524288]{0:T(1024)(128)(4,1)S(1)}, s32[]{:S(2)}) async-start(s8[4718592]{0:T(1024)(128)(4,1)} %bitcast.296), calls=%async_computation.9 | async-start | bytes 1048576
  66.5 37.7 %copy-start.52 = (f32[768]{0:T(1024)S(1)}, f32[768]{0:T(1024)}, u32[]{:S(2)}) copy-start(f32[768]{0:T(1024)} %param.35) | copy-start | bytes 9220
  104.1 5.5 copy-start.53
  104.2 6.1 copy-start.36
  104.2 6.1 copy-start.46
  109.6 2.4 copy-start.7
  110.2 3.0 copy-start.34
  110.2 2.9 copy-start.28
  115.1 3.4 copy-start.21
  115.8 2.0 copy-start.19
  163.8 2.2 copy-start.9
  202.6 8.4 copy-start.22
  218.5 135.6 %reduce-scatter.5.cloned.1.call-start = ((), (), s32[]{:S(2)}) async-start(), calls=%async_computation.3 | async-start | bytes 835584 | tf_op jit(solution)/shard_map/reduce_scatter | solution.py:213
  219.0 15.3 %copy-start.10 = (f32[256,768]{1,0:T(8,128)S(1)}, f32[256,768]{1,0:T(8,128)}, u32[]{:S(2)}) copy-start(f32[256,768]{1,0:T(8,128)} %copy-done.9) | copy-start | bytes 2359300
  219.0 15.3 %copy-start.38 = (f32[256]{0:T(256)S(1)}, f32[256]{0:T(256)}, u32[]{:S(2)}) copy-start(f32[256]{0:T(256)} %add_rsqrt_fusion.3) | copy-start | bytes 3076
  219.0 15.5 %copy-start.16 = (bf16[256,768]{1,0:T(8,128)(2,1)S(1)}, bf16[256,768]{1,0:T(8,128)(2,1)}, u32[]{:S(2)}) copy-start(bf16[256,768]{1,0:T(8,128)(2,1)} %copy-done.15) | copy-start | bytes 1179652
  219.0 15.5 %copy-start.45 = (f32[256]{0:T(256)S(1)}, f32[256]{0:T(256)}, u32[]{:S(2)}) copy-start(f32[256]{0:T(256)} %add_rsqrt_fusion.4) | copy-start | bytes 3076
  235.6 698.6 %all-reduce.12.cloned.1.call-start = ((), (), s32[]{:S(2)}) async-start(), calls=%async_computation.4 | async-start | bytes 56623104 | tf_op jit(solution)/shard_map/psum | solution.py:268
  354.1 3.0 copy-start.8
  354.1 5.3 copy-start.35
  354.1 5.3 copy-start.29
  354.1 5.3 copy-start.37
  361.0 2.4 copy-start.14
  361.0 2.4 copy-start.50
  363.4 18.9 %copy-start.12 = (f32[1024,768]{1,0:T(8,128)S(1)}, f32[1024,768]{1,0:T(8,128)}, u32[]{:S(2)}) copy-start(f32[1024,768]{1,0:T(8,128)} %copy-done.11) | copy-start | bytes 9437188
  363.4 18.9 %copy-start.27 = (f32[768]{0:T(1024)S(1)}, f32[768]{0:T(1024)}, u32[]{:S(2)}) copy-start(f32[768]{0:T(1024)} %param.30) | copy-start | bytes 9220
  382.3 10.8 %copy-start.17 = (bf16[1024,3072]{1,0:T(8,128)(2,1)S(1)}, bf16[1024,3072]{1,0:T(8,128)(2,1)}, u32[]{:S(2)}) copy-start(bf16[1024,3072]{1,0:T(8,128)(2,1)} %get-tuple-element.272) | copy-start | bytes 18874372
  382.3 10.8 %copy-start.31 = (f32[768]{0:T(1024)S(1)}, f32[768]{0:T(1024)}, u32[]{:S(2)}) copy-start(f32[768]{0:T(1024)} %param.31) | copy-start | bytes 9220
  393.0 8.5 copy-start.33
  403.2 5.4 copy-start.13
  403.2 2.5 copy-start.47
  403.2 5.4 copy-start.39
  404.2 4.5 copy-start.48
  405.8 5.5 slice-start.5
  408.7 2.7 copy-start.20
  408.7 2.6 slice-start.6
  427.5 5.1 copy-start.1
  427.5 1.9 copy-start.5
  439.7 7.1 copy-start.2
  460.2 5.1 copy-start.1
  460.3 1.9 copy-start.5
  472.5 7.1 copy-start.2
  501.2 46.0 %copy-start.41 = (f32[768]{0:T(1024)S(1)}, f32[768]{0:T(1024)}, u32[]{:S(2)}) copy-start(f32[768]{0:T(1024)} %get-tuple-element.273) | copy-start | bytes 9220
  501.2 46.0 %copy-start.42 = (f32[768]{0:T(1024)S(1)}, f32[768]{0:T(1024)}, u32[]{:S(2)}) copy-start(f32[768]{0:T(1024)} %get-tuple-element.223) | copy-start | bytes 9220
  501.2 45.9 %copy-start.43 = (f32[768]{0:T(1024)S(1)}, f32[768]{0:T(1024)}, u32[]{:S(2)}) copy-start(f32[768]{0:T(1024)} %get-tuple-element.225) | copy-start | bytes 9220
  501.3 86.3 %copy-start.40 = (f32[1024]{0:T(1024)S(1)}, f32[1024]{0:T(1024)}, u32[]{:S(2)}) copy-start(f32[1024]{0:T(1024)} %copy-done.39) | copy-start | bytes 12292
  942.2 12.1 %slice-start = ((s8[9437184]{0:T(1024)(128)(4,1)}), s8[4194304]{0:T(1024)(128)(4,1)S(1)}, s32[]{:S(2)}) async-start(s8[9437184]{0:T(1024)(128)(4,1)} %bitcast.286), calls=%async_computation.5 | async-start | bytes 8388608
  945.6 8.8 slice-start.1
  945.6 8.8 slice-start.2
  (9 other events, 12.4 us)
Sparse Core Ops, SparseCore 0:
  218.6 3.4 reduce-scatter.2
  235.8 118.2 reduce-scatter.4
  501.3 432.8 all-reduce.11
where the time goes:
time: 976 us; the launch traced here: 965 us
  waiting for transfers between devices  457 us (47%)
  matrix products  200 us (20%)
  blocking collectives  134 us (14%)
  other arithmetic  83.3 us (9%)
  local copies, waits for them, and re-layouts  73.8 us (8%)
  between operations  15.3 us (2%)
    psum x1, waiting for transfers between devices, on_device(): lax.psum((grad_attn_weight, grad_query_bias, grad_value_bias, grad_merge_...  338 us
    reduce_scatter x1, waiting for transfers between devices, on_device(): lax.psum_scatter(grad_col, 'wide', scatter_dimension=0, tiled=True)  118 us
    all_gather x1, blocking collectives, on_device(): lax.all_gather(span_pooled_code, 'wide', axis=0, tiled=True)  44.5 us
    psum x1, blocking collectives, on_device(): loss = lax.psum(jnp.sum(log_total - hits), 'wide')  42.1 us
    dot_general x4, matrix products, right_dot(): lax.dot_general(left, right, (((1,), (1,)), ((), ())), preferred_element_...  40.5 us
    psum x1, blocking collectives, on_device(): lax.psum((grad_attn_weight, grad_query_bias, grad_value_bias, grad_merge_...  40.4 us
    dot_general x1, matrix products, on_device(): jnp.dot(normed_low, perceptron_entry_kernel, preferred_element_type=jnp.f...  37.6 us
    dot_general x4, matrix products, left_dot(): lax.dot_general(left, right, (((0,), (0,)), ((), ())), preferred_element_...  28.8 us
  transfers between devices with their start and end apart: 3, of which 2 were waited for; matrix products, arithmetic and copies ran while one was open for 3% of the time, Pallas kernels for 0%

commit v1 on v0

--- a/solution.py
+++ b/solution.py
@@ -3,22 +3,191 @@
 import jax
 import jax.numpy as jnp
 from jax import lax
+from jax.experimental import pallas as pl
+from jax.experimental.pallas import tpu as pltpu
 from jax.sharding import PartitionSpec as P
 
 HEADS = 12
 S_ROW = 8
-
-
+BOTH = ("wide", "narrow")
+BF = jnp.bfloat16
+F32 = jnp.float32
 HIGHEST = lax.Precision.HIGHEST
 
 
-def joined(value, axis, join):
-    pieces = jax.tree.map(lambda part: lax.all_gather(part, axis), value)
-    head = jax.tree.map(lambda part: part[0], pieces)
-    tail = jax.tree.map(lambda part: part[1:], pieces)
-    total, _ = lax.scan(lambda total, section: (join(total, section), None), head, tail)
+class Place:
+    def __init__(self):
+        self.wide, self.narrow = lax.axis_size("wide"), lax.axis_size("narrow")
+        self.count = self.wide * self.narrow
+        self.core = lax.axis_index("narrow")
+        self.me = lax.axis_index("wide") * self.narrow + self.core
+        bits = [self.narrow << i for i in range(self.wide.bit_length() - 1)]
+        swapped = bits[:2][::-1] + bits[2:]
+        self.steps = [(1, 1)] + list(zip(bits, swapped))
+
+    def exchange(self, value, step):
+        pairs = [(i, i ^ step[i % 2]) for i in range(self.count)]
+        return lax.ppermute(value, BOTH, pairs)
+
+    def bit(self, step):
+        if step[0] == step[1]:
+            return (self.me // step[0]) % 2
+        return jnp.where(self.core == 0, (self.me // step[0]) % 2, (self.me // step[1]) % 2)
+
+
+def scatter_step(total, step, place):
+    half = total.shape[0] // 2
+    bit = place.bit(step)
+    keep = lax.dynamic_slice_in_dim(total, bit * half, half)
+    send = lax.dynamic_slice_in_dim(total, (1 - bit) * half, half).astype(BF)
+    return keep.astype(F32) + place.exchange(send, step).astype(F32)
+
+
+def gather_step(part, step, place):
+    bit = place.bit(step)
+    got = place.exchange(part, step)
+    return jnp.where(bit == 0, jnp.concatenate([part, got]), jnp.concatenate([got, part]))
+
+
+def sum_everywhere(total, place):
+    for step in place.steps:
+        total = scatter_step(total, step, place)
+    part = total.astype(BF)
+    for step in place.steps[::-1]:
+        part = gather_step(part, step, place)
+    return part.astype(F32)
+
+
+def sum_small(total, place):
+    for step in place.steps:
+        total = total + place.exchange(total, step)
     return total
 
+
+def nt_dot(left, right, precision=None):
+    return lax.dot_general(
+        left, right, (((1,), (1,)), ((), ())), precision=precision, preferred_element_type=F32
+    )
+
+
+def contrast_kernel(block, me_ref, cool_ref, all_ref, own_ref, ids_row_ref, ids_col_ref, partner_row_ref,
+                    partner_col_ref, partner_own_ref, loss_ref, grad_ref, sums_ref, rnorm_ref):
+    count, width_all = all_ref.shape
+    owned = own_ref.shape[0]
+    widths = [width_all * f // 12 for f in (1, 2, 4, 8, 12)]
+    warm = 1.0 / cool_ref[0]
+    ones = jnp.ones((8, 1), F32)
+    lane = lax.broadcasted_iota(jnp.int32, (1, 128), 1)
+    first_mask = (lane < widths[0]).astype(F32)
+
+    def spans():
+        return [(0, 128, True), (0, 128, False), (128, widths[2], False),
+                (widths[2], widths[3], False), (widths[3], widths[4], False)]
+
+    squares = jnp.zeros((8, count), F32)
+    for index, (lo, hi, masked) in enumerate(spans()):
+        part = all_ref[:, lo:hi].astype(F32)
+        if masked:
+            part = part * first_mask
+        term = nt_dot(jnp.ones((8, hi - lo), F32), part * part, HIGHEST)
+        squares = term if index <= 1 else squares + term
+        rnorm_ref[index] = lax.rsqrt(squares[:1] + 1e-06)
+    sums_ref[...] = jnp.zeros_like(sums_ref)
+    col = ids_row_ref[...]
+    hits = jnp.zeros((1, 1), F32)
+    for b in range(count // block):
+        rows = pl.ds(b * block, block)
+        diagonal = ids_col_ref[rows, :] == col
+        positive = partner_col_ref[rows, :] == col
+        gram = jnp.zeros((block, count), F32)
+        norms = jnp.zeros((block, 1), F32)
+        for index, (lo, hi, masked) in enumerate(spans()):
+            mine = all_ref[rows, lo:hi]
+            if masked:
+                mine = mine * first_mask.astype(BF)
+            wide = mine.astype(F32)
+            term = nt_dot(mine, all_ref[:, lo:hi])
+            square = jnp.sum(wide * wide, axis=1, keepdims=True)
+            gram, norms = (term, square) if index <= 1 else (gram + term, norms + square)
+            scores = gram * (lax.rsqrt(norms + 1e-06) * warm) * rnorm_ref[index]
+            sums_ref[index] += jnp.sum(
+                jnp.where(diagonal, 0.0, jnp.exp(scores)), axis=0, keepdims=True
+            )
+            hits += jnp.sum(
+                jnp.sum(jnp.where(positive, scores, 0.0), axis=0, keepdims=True), axis=1, keepdims=True
+            )
+    logs = jnp.zeros((1, count), F32)
+    for index in range(5):
+        logs += jnp.log(sums_ref[index])
+    loss_ref[...] = jnp.sum(logs, axis=1, keepdims=True) - hits
+
+    first = me_ref[0] * owned
+    orow = lax.broadcasted_iota(jnp.int32, (owned, count), 0) + first
+    diagonal = orow == col
+    picks = (partner_own_ref[...] == col).astype(F32) + (partner_row_ref[...] == orow).astype(F32)
+    gram = jnp.zeros((owned, count), F32)
+    norms = jnp.zeros((owned, 1), F32)
+    weights, inverses = [], []
+    for index, (lo, hi, masked) in enumerate(spans()):
+        mine = own_ref[:, lo:hi]
+        if masked:
+            mine = mine * first_mask.astype(BF)
+        wide = mine.astype(F32)
+        term = nt_dot(mine, all_ref[:, lo:hi])
+        square = jnp.sum(wide * wide, axis=1, keepdims=True)
+        gram, norms = (term, square) if index <= 1 else (gram + term, norms + square)
+        inverse = lax.rsqrt(norms + 1e-06)
+        raised = jnp.where(diagonal, 0.0, jnp.exp(gram * (inverse * warm) * rnorm_ref[index]))
+        own_sum = jnp.sum(raised, axis=1, keepdims=True)
+        pull = raised * (1.0 / own_sum + 1.0 / sums_ref[index]) - picks
+        weights.append(pull * (rnorm_ref[index] * warm))
+        inverses.append(inverse)
+    stack = jnp.concatenate(weights, axis=0)
+    top = stack.astype(BF)
+    rest = stack - top.astype(F32)
+    middle = rest.astype(BF)
+    low = (rest - middle.astype(F32)).astype(BF)
+    parts = jnp.dot(
+        jnp.concatenate([top, middle, low], axis=0), all_ref[...], preferred_element_type=F32
+    )
+    unit_grads = parts[: 5 * owned] + parts[5 * owned : 10 * owned] + parts[10 * owned :]
+    total = jnp.zeros((owned, width_all), F32)
+    column = lax.broadcasted_iota(jnp.int32, (owned, width_all), 1)
+    embed = own_ref[...].astype(F32)
+    for index in range(5):
+        inside = column < widths[index]
+        mine = jnp.where(inside, embed, 0.0)
+        grad = jnp.where(inside, unit_grads[index * owned : (index + 1) * owned], 0.0)
+        along = jnp.sum(mine * grad, axis=1, keepdims=True)
+        inverse = inverses[index]
+        total += inverse * grad - (inverse * inverse * inverse * along) * mine
+    grad_ref[...] = total
+
+
+def contrast(everyone, own, partner, coolness, place):
+    count, width = everyone.shape
+    owned = own.shape[0]
+    block = min(count, 256)
+    bits = len(place.steps)
+    ids = jnp.arange(count, dtype=jnp.int32).reshape([2] * bits + [owned])
+    ids = ids.transpose(list(range(bits))[::-1] + [bits]).reshape(count)
+    partner_there = partner[ids]
+    own_partner = lax.dynamic_slice_in_dim(partner, place.me * owned, owned)
+    whole = pl.BlockSpec(memory_space=pltpu.VMEM)
+    smem = pl.BlockSpec(memory_space=pltpu.SMEM)
+    return pl.pallas_call(
+        partial(contrast_kernel, block),
+        out_shape=(
+            jax.ShapeDtypeStruct((1, 1), F32),
+            jax.ShapeDtypeStruct((owned, width), F32),
+        ),
+        in_specs=[smem, smem] + [whole] * 7,
+        out_specs=(whole, whole),
+        scratch_shapes=[pltpu.VMEM((5, 1, count), F32), pltpu.VMEM((5, 1, count), F32)],
+        compiler_params=pltpu.CompilerParams(vmem_limit_bytes=56 * 1024 * 1024),
+        name="contrast",
+    )(place.me.reshape(1), coolness, everyone, own, ids[None, :], ids[:, None],
+      partner_there[None, :], partner_there[:, None], own_partner[:, None])
 
 def layer_norm(values, gain, shift):
     center = values - jnp.mean(values, axis=-1, keepdims=True)
@@ -90,35 +259,6 @@
     )
     stacked = jnp.stack([grad_queries, grad_keys, grad_values], axis=1)
     return stacked.reshape(length, 3 * width).astype(jnp.bfloat16)
-
-
-def tile_logits(source_vector_code, target_vector_code, softmax_coolness, self_pair_filter):
-    width_all = source_vector_code.shape[1]
-    stacks = []
-    for factor in (12, 8, 4, 2, 1):
-        width = width_all * factor // 12
-        row_part = source_vector_code[:, :width]
-        col_part = target_vector_code[:, :width]
-        row_unit = row_part * lax.rsqrt(jnp.sum(row_part * row_part, axis=1, keepdims=True) + 1e-06)
-        col_unit = col_part * lax.rsqrt(jnp.sum(col_part * col_part, axis=1, keepdims=True) + 1e-06)
-        cosine_logits = (
-            lax.dot_general(
-                row_unit,
-                col_unit,
-                (((1,), (1,)), ((), ())),
-                precision=HIGHEST,
-                preferred_element_type=jnp.float32,
-            )
-            / softmax_coolness[0]
-        )
-        stacks.append(jnp.where(self_pair_filter, -1000000000.0, cosine_logits))
-    return jnp.stack(stacks)
-
-
-def combine_stats(first, second):
-    top = jnp.maximum(first[0], second[0])
-    summed = first[1] * jnp.exp(first[0] - top) + second[1] * jnp.exp(second[0] - top)
-    return (top, summed, first[2] + second[2])
 
 
 def on_device(
@@ -182,35 +322,13 @@
         / counts[..., None]
     )
     span_pooled_code = pooled.reshape(seg_dev, width).astype(jnp.bfloat16)
-    wide_index = lax.axis_index("wide")
-    narrow_index = lax.axis_index("narrow")
-    wide_size = lax.axis_size("wide")
-    narrow_size = lax.axis_size("narrow")
-    source_vector_code = lax.all_gather(span_pooled_code, "narrow", axis=0, tiled=True)
-    target_vector_code = lax.all_gather(span_pooled_code, "wide", axis=0, tiled=True)
-    tile_rows = narrow_size * seg_dev
-    row_ids = wide_index * tile_rows + jnp.arange(tile_rows, dtype=jnp.int32)
-    col_local = jnp.arange(wide_size * seg_dev, dtype=jnp.int32)
-    col_ids = (col_local // seg_dev * narrow_size + narrow_index) * seg_dev + col_local % seg_dev
-    row_positive = lax.dynamic_slice_in_dim(partner_global_index, wide_index * tile_rows, tile_rows)
-    self_pair_filter = row_ids[:, None] == col_ids[None, :]
-    hit_mask = row_positive[:, None] == col_ids[None, :]
-    cosine_logits, tile_back = jax.vjp(
-        partial(tile_logits, softmax_coolness=softmax_coolness, self_pair_filter=self_pair_filter),
-        source_vector_code.astype(jnp.float32),
-        target_vector_code.astype(jnp.float32),
-    )
-    top = jnp.max(cosine_logits, axis=2)
-    summed = jnp.sum(jnp.exp(cosine_logits - top[..., None]), axis=2)
-    hits = jnp.sum(jnp.where(hit_mask[None], cosine_logits, 0.0), axis=2)
-    top, summed, hits = joined((top, summed, hits), "narrow", combine_stats)
-    log_total = top + jnp.log(summed)
-    loss = lax.psum(jnp.sum(log_total - hits), "wide")
-    grad_scores = jnp.exp(cosine_logits - log_total[..., None]) - hit_mask[None].astype(jnp.float32)
-    grad_row, grad_col = tile_back(grad_scores)
-    grad_embed = lax.psum_scatter(
-        grad_row, "narrow", scatter_dimension=0, tiled=True
-    ) + lax.psum_scatter(grad_col, "wide", scatter_dimension=0, tiled=True)
+    place = Place()
+    everyone = span_pooled_code
+    for step in [(m, m) for m in (s[0] for s in place.steps[::-1])]:
+        everyone = gather_step(everyone, step, place)
+    loss, grad_embed = contrast(
+        everyone, span_pooled_code, partner_global_index, softmax_coolness, place
+    )
     per_segment = grad_embed.reshape(row_count, S_ROW, width) / counts[..., None]
     grad_output = jnp.einsum("rls,rsd->rld", onehot, per_segment, precision=HIGHEST).reshape(
         row_count * length, width
@@ -224,24 +342,6 @@
     grad_inner_weight = left_dot(normed_low, grad_inner)
     grad_inner_bias = jnp.sum(grad_inner.astype(jnp.float32), axis=0)
     grad_normed = grad_second + right_dot(grad_inner, perceptron_entry_kernel)
-    (
-        grad_inner_weight,
-        grad_inner_bias,
-        grad_outer_weight,
-        grad_outer_bias,
-        grad_second_gain,
-        grad_second_shift,
-    ) = lax.psum(
-        (
-            grad_inner_weight,
-            grad_inner_bias,
-            grad_outer_weight,
-            grad_outer_bias,
-            grad_second_gain,
-            grad_second_shift,
-        ),
-        ("wide", "narrow"),
-    )
     grad_first, grad_first_gain, grad_first_shift = first_back(grad_normed)
     grad_attn = grad_first.astype(jnp.bfloat16)
     grad_merge_weight = left_dot(mixed, grad_attn)
@@ -257,26 +357,26 @@
     grad_query_bias = bias_sums[:width]
     grad_value_bias = bias_sums[2 * width :]
     input_grad = grad_first + right_dot(grad_packed, triple_kernel_panel)
+    small = [
+        grad_query_bias, grad_value_bias, grad_merge_bias, grad_first_gain, grad_first_shift,
+        grad_inner_bias, grad_outer_bias, grad_second_gain, grad_second_shift,
+    ]
+    sizes = [v.shape[0] for v in small]
+    small = jnp.concatenate(small)
+    small = jnp.pad(small, (0, -small.shape[0] % (place.count * 128))).reshape(place.count, -1)
+    grad_outer_weight = sum_everywhere(grad_outer_weight, place)
+    grad_inner_weight = sum_everywhere(grad_inner_weight, place)
+    merged = sum_everywhere(jnp.concatenate([grad_attn_weight, grad_merge_weight], axis=1), place)
+    grad_attn_weight, grad_merge_weight = merged[:, : 3 * width], merged[:, 3 * width :]
+    small = sum_small(small, place).reshape(-1)
+    cuts, at = [], 0
+    for size in sizes:
+        cuts.append(small[at : at + size])
+        at += size
     (
-        grad_attn_weight,
-        grad_query_bias,
-        grad_value_bias,
-        grad_merge_weight,
-        grad_merge_bias,
-        grad_first_gain,
-        grad_first_shift,
-    ) = lax.psum(
-        (
-            grad_attn_weight,
-            grad_query_bias,
-            grad_value_bias,
-            grad_merge_weight,
-            grad_merge_bias,
-            grad_first_gain,
-            grad_first_shift,
-        ),
-        ("wide", "narrow"),
-    )
+        grad_query_bias, grad_value_bias, grad_merge_bias, grad_first_gain, grad_first_shift,
+        grad_inner_bias, grad_outer_bias, grad_second_gain, grad_second_shift,
+    ) = cuts
     return (
         loss.reshape(1),
         layer_out,

time: 976 us -> 569 us (0.58)
  waiting for transfers between devices: 457 us -> 151 us
  blocking collectives: 134 us -> 0 us
  starting transfers between devices: 0.59 us -> 43.9 us
  matrix products: 200 us -> 171 us
  other arithmetic: 83.3 us -> 99 us
  between operations: 15.3 us -> 2.78 us
  local copies, waits for them, and re-layouts: 73.8 us -> 84.7 us
    psum x1 -> x0, waiting for transfers between devices: 338 us -> none  [on_device(): lax.psum((grad_attn_weight, grad_query_bias, grad_value_bias, grad_merge_...]
    ppermute x0 -> x40, waiting for transfers between devices: none -> 151 us  [exchange(): return lax.ppermute(value, BOTH, pairs)]
    reduce_scatter x2 -> x0, waiting for transfers between devices: 118 us -> none  [the longest x1 118 us: on_device(): lax.psum_scatter(grad_col, 'wide', scatter_dimension=0, tiled=True)]
    psum x2 -> x0, blocking collectives: 82.5 us -> none  [the longest x1 42.1 us: on_device(): loss = lax.psum(jnp.sum(log_total - hits), 'wide')]
    all_gather x5 -> x0, blocking collectives: 51.9 us -> none  [the longest x1 44.5 us: on_device(): lax.all_gather(span_pooled_code, 'wide', axis=0, tiled=True)]
    ppermute x0 -> x40, starting transfers between devices: none -> 43.9 us  [exchange(): return lax.ppermute(value, BOTH, pairs)]
    dot_general x15 -> x0, matrix products: 26.8 us -> none  [tile_logits(): lax.dot_general(row_unit, col_unit, (((1,), (1,)), ((), ())), precision=H...]
    select_n x0 -> x18, other arithmetic: none -> 23.5 us  [the longest x17 22.8 us: gather_step(): jnp.where(bit == 0, jnp.concatenate([part, got]), jnp.concatenate([got, p...]
  transfers between devices with their start and end apart: 3 -> 40, of which waited for: 2 -> 22; matrix products, arithmetic and copies ran while one was open for 3% -> 17% of each run, Pallas kernels for 0% -> 0%
where the time goes in v1:
time: 569 us; the launch traced here: 559 us
  matrix products  171 us (30%)
  waiting for transfers between devices  151 us (27%)
  other arithmetic  99 us (17%)
  local copies, waits for them, and re-layouts  84.7 us (15%)
  starting transfers between devices  43.9 us (8%)
  Pallas kernels  6.3 us (1%)
    ppermute x40, waiting for transfers between devices, exchange(): return lax.ppermute(value, BOTH, pairs)  151 us
    ppermute x40, starting transfers between devices, exchange(): return lax.ppermute(value, BOTH, pairs)  43.9 us
    dot_general x4, matrix products, right_dot(): lax.dot_general(left, right, (((1,), (1,)), ((), ())), preferred_element_...  40.6 us
    dot_general x1, matrix products, on_device(): jnp.dot(normed_low, perceptron_entry_kernel, preferred_element_type=jnp.f...  35 us
    dot_general x4, matrix products, left_dot(): lax.dot_general(left, right, (((0,), (0,)), ((), ())), preferred_element_...  28.7 us
    select_n x17, other arithmetic, gather_step(): jnp.where(bit == 0, jnp.concatenate([part, got]), jnp.concatenate([got, p...  22.8 us
    convert_element_type x3, other arithmetic, sum_everywhere(): return part.astype(F32)  22.7 us
    convert_element_type x2, other arithmetic, attend_back(): grad_raw = (probs * (grad_probs - inner_sum)).astype(jnp.bfloat16)  14.3 us
  transfers between devices with their start and end apart: 40, of which 22 were waited for; matrix products, arithmetic and copies ran while one was open for 17% of the time, Pallas kernels for 0%

profile of v1, /device:TPU:0, one launch (start us, length us, event | category | flops | bytes accessed | tf_op | source)
XLA Modules:
  0.0 559.2 jit_solution(11804735199772637617)
XLA Ops:
  2.9 7.3 %add_convert_fusion.1 = bf16[1024,2304]{1,0:T(8,128)(2,1)} fusion(bf16[1024,768]{1,0:T(8,128)(2,1)} %param.21, bf16[768,2304]{1,0:T(8,128)(2,1)S(1)} %copy-done, f32[2304]{0:T(1024)S(1)} %pad_maximum_fusion.1), kind=kOutput, calls=%fused_computation.68 | convolution fusion | flops 3628597248 | bytes 9839616 | tf_op jit(solution)/shard_map/dot_general | solution.py:289
  10.2 6.6 %copy.90 = bf16[2,512,2304]{1,2,0:T(8,128)(2,1)} copy(bf16[2,512,2304]{2,1,0:T(8,128)(2,1)} %bitcast.173) | data formatting | bytes 9437184 | tf_op jit(solution)/shard_map/while | solution.py:293
  16.8 36.7 %while.22 = (s32[]{:T(128)}, bf16[2,512,768]{2,1,0:T(8,128)(2,1)}, f32[2,12,512,1]{2,1,3,0:T(8,128)}, bf16[2,512,2304]{1,2,0:T(8,128)(2,1)}, s32[2,512]{1,0:T(2,128)S(1)}, /*index=5*/s32[]{:T(128)}) while((s32[]{:T(128)}, bf16[2,512,768]{2,1,0:T(8,128)(2,1)}, f32[2,12,512,1]{2,1,3,0:T(8,128)}, bf16[2,512,2304]{1,2,0:T(8,128)(2,1)}, ...), condition=%wide.region_3.4_spmd, body=%wide.region_0.3_spmd.sunk | while | flops 843704320 | bytes 60913868 | solution.py:293
  21.1 3.5 fusion.100
  24.7 5.5 fusion.101
  30.8 2.3 copy.111
  39.5 3.5 fusion.100
  43.0 5.5 fusion.101
  49.2 2.3 copy.111
  53.6 3.9 fusion.55
  59.2 35.0 %multiply_convert_fusion.3 = (bf16[1024,3072]{1,0:T(8,128)(2,1)S(1)}, f32[1024,3072]{1,0:T(8,128)}, f32[1024,3072]{1,0:T(8,128)}) fusion(f32[3072]{0:T(1024)S(1)} %copy-done.52, bf16[768,3072]{1,0:T(8,128)(2,1)S(1)} %bitcast.182, f32[1024,768]{1,0:T(8,128)S(1)} %get-tuple-element.211, f32[768]{0:T(1024)S(1)} %copy-done.30, f32[768]{0:T(1024)S(1)} %copy-done.26, ...), kind=kOutput, calls=%fused_computation.49 | convolution fusion | flops 5043388416 | bytes 39348224 | tf_op jit(solution)/shard_map/dot_general | solution.py:303
  94.2 5.4 fusion.56
  104.0 4.0 collective-permute-start
  113.5 2.5 collective-permute-done.1
  119.6 3.0 collective-permute-done.2
  126.9 3.4 collective-permute-done.3
  140.5 5.0 gather_fusion
  147.0 2.6 maximum_select_fusion.9.all_ref
  149.6 6.3 %contrast.1 = (f32[1,1]{1,0:T(1,128)}, f32[16,768]{1,0:T(8,128)}) custom-call(s32[1]{0:T(128)} %bitcast.22.me_ref, f32[1]{0:T(128)S(6)} %copy.140.cool_ref, bf16[512,768]{1,0:T(8,128)(2,1)} %maximum_select_fusion.9.all_ref, bf16[16,768]{1,0:T(8,128)(2,1)} %fusion.39.own_ref, s32[1,512]{1,0:T(1,128)} %reshape.627.ids_row_ref, s32[512,1]{1,0:T(8,128)} %copy.92.ids_col_ref, ...), custom_call_target="tpu_custom_call" | custom-call | tf_op jit(solution)/shard_map/contrast/pallas_call | solution.py:178
  155.9 2.9 fusion.57
  164.3 18.8 %convert_reduce_fusion = (f32[3072]{0:T(1024)}, bf16[1024,3072]{1,0:T(8,128)(2,1)}) fusion(f32[1024,3072]{1,0:T(8,128)} %get-tuple-element.197, bf16[1024,768]{1,0:T(8,128)(2,1)} %get-tuple-element.187, bf16[3072,768]{1,0:T(8,128)(2,1)} %param.34, f32[1024,3072]{1,0:T(8,128)} %get-tuple-element.212, f32[3072]{0:T(1024)S(1)} %copy-done.53), kind=kOutput, calls=%fused_computation.47 | convolution fusion | flops 4885312512 | bytes 37773312 | tf_op jit(solution)/shard_map/dot_general | solution.py:205
  183.1 11.2 %multiply_reduce_fusion.1 = (f32[768]{0:T(1024)}, f32[1024]{0:T(1024)S(1)}, f32[768]{0:T(1024)}, f32[1024,768]{1,0:T(8,128)S(1)}) fusion(f32[1024,768]{1,0:T(8,128)S(1)} %copy-done.11, f32[1024]{0:T(1024)S(1)} %fusion.44, f32[1024]{0:T(1024)S(1)} %broadcast_multiply_fusion.1, f32[768]{0:T(1024)S(1)} %copy-done.27, ...), kind=kOutput, calls=%fused_computation.90 | convolution fusion | flops 4839699456 | bytes 20472832 | tf_op jit(solution)/shard_map/dot_general | solution.py:205
  194.4 8.5 %fusion.46 = f32[768,3072]{1,0:T(8,128)} fusion(bf16[1024,3072]{1,0:T(8,128)(2,1)S(1)} %copy-done.18, f32[1024,768]{1,0:T(8,128)S(1)} %copy-done.11, f32[768]{0:T(1024)S(1)} %copy-done.31, f32[768]{0:T(1024)S(1)} %copy-done.27, f32[1024]{0:T(1024)S(1)} %fusion.44, f32[1024]{0:T(1024)S(1)} %broadcast_multiply_fusion.1), kind=kOutput, calls=%fused_computation.181 | convolution fusion | flops 4835770368 | bytes 18888704 | tf_op jit(solution)/shard_map/dot_general | solution.py:199
  206.9 2.9 fusion.58
  209.8 2.6 convolution_convert_fusion
  212.4 65.6 %while.23 = (s32[]{:T(128)}, bf16[2,512,2304]{1,2,0:T(8,128)(2,1)}, bf16[2,512,2304]{1,2,0:T(8,128)(2,1)}, s32[2,512]{1,0:T(2,128)S(1)}, f32[2,12,512,1]{2,1,3,0...) while((s32[]{:T(128)}, bf16[2,512,2304]{1,2,0:T(8,128)(2,1)}, bf16[2,512,2304]{1,2,0:T(8,128)(2,1)}, ...), condition=%wide.region_15.16_spmd, body=%wide.region_13.15_spmd.sunk | while | flops 2065033216 | bytes 143939856 | solution.py:350
  216.9 2.3 copy.112
  223.0 3.1 fusion.108
  226.1 7.1 %multiply_reduce_fusion.7 = (f32[12,512]{1,0:T(8,128)S(1)}, f32[12,512,512]{1,2,0:T(8,128)}) fusion(f32[12,512,512]{1,2,0:T(8,128)S(1)} %fusion.107, f32[12,512]{1,0:T(8,128)S(1)} %copy-done.19, pred[512,512]{0,1:T(8,128)(4,1)S(1)} %copy-done.6, bf16[512,12,64]{0,2,1:T(8,128)(2,1)S(1)} %bitcast.165, bf16[512,3,12,64]{0,3,2,1:T(8,128)(2,1)S(1)} %bitcast.158), kind=kOutput, calls=%fused_computation.20.clone.1 | convolution fusion | flops 418375680 | bytes 27058176 | tf_op jit(solution)/shard_map/while/body/eval_jaxpr/qhd,khd->hqk/dot_general | solution.py:243
  233.2 7.1 %multiply_convert_fusion.5 = bf16[12,512,512]{1,2,0:T(8,128)(2,1)S(1)} fusion(f32[12,512,512]{1,2,0:T(8,128)} %get-tuple-element.294, f32[12,512,512]{1,2,0:T(8,128)S(1)} %fusion.107, f32[12,512]{1,0:T(8,128)S(1)} %get-tuple-element.295, f32[12,512]{1,0:T(8,128)S(1)} %copy-done.19, pred[512,512]{0,1:T(8,128)(4,1)S(1)} %copy-done.6), kind=kLoop, calls=%fused_computation.19.clone.1 | loop fusion | flops 18874368 | bytes 31768576 | tf_op jit(solution)/shard_map/while/body/eval_jaxpr/convert_element_type | solution.py:250
  249.6 2.3 copy.112
  255.7 3.1 fusion.108
  258.9 7.1 %multiply_reduce_fusion.7 = (f32[12,512]{1,0:T(8,128)S(1)}, f32[12,512,512]{1,2,0:T(8,128)}) fusion(f32[12,512,512]{1,2,0:T(8,128)S(1)} %fusion.107, f32[12,512]{1,0:T(8,128)S(1)} %copy-done.19, pred[512,512]{0,1:T(8,128)(4,1)S(1)} %copy-done.6, bf16[512,12,64]{0,2,1:T(8,128)(2,1)S(1)} %bitcast.165, bf16[512,3,12,64]{0,3,2,1:T(8,128)(2,1)S(1)} %bitcast.158), kind=kOutput, calls=%fused_computation.20.clone.1 | convolution fusion | flops 418375680 | bytes 27058176 | tf_op jit(solution)/shard_map/while/body/eval_jaxpr/qhd,khd->hqk/dot_general | solution.py:243
  265.9 7.1 %multiply_convert_fusion.5 = bf16[12,512,512]{1,2,0:T(8,128)(2,1)S(1)} fusion(f32[12,512,512]{1,2,0:T(8,128)} %get-tuple-element.294, f32[12,512,512]{1,2,0:T(8,128)S(1)} %fusion.107, f32[12,512]{1,0:T(8,128)S(1)} %get-tuple-element.295, f32[12,512]{1,0:T(8,128)S(1)} %copy-done.19, pred[512,512]{0,1:T(8,128)(4,1)S(1)} %copy-done.6), kind=kLoop, calls=%fused_computation.19.clone.1 | loop fusion | flops 18874368 | bytes 31768576 | tf_op jit(solution)/shard_map/while/body/eval_jaxpr/convert_element_type | solution.py:250
  278.0 6.8 %copy.97 = bf16[2,512,2304]{2,1,0:T(8,128)(2,1)} copy(bf16[2,512,2304]{1,2,0:T(8,128)(2,1)} %get-tuple-element.82) | data formatting | bytes 9437184 | tf_op jit(solution)/shard_map/while | solution.py:350
  284.8 7.2 %convolution_bitcast_fusion = f32[768,2304]{1,0:T(8,128)S(1)} fusion(bf16[1024,2304]{1,0:T(8,128)(2,1)} %bitcast.171, bf16[1024,768]{1,0:T(8,128)(2,1)} %param.21), kind=kOutput, calls=%fused_computation.69 | convolution fusion | flops 3623878656 | bytes 13369344 | tf_op jit(solution)/shard_map/dot_general | solution.py:199
  296.0 10.1 %fusion.59 = f32[3072,768]{1,0:T(8,128)} fusion(bf16[1024,3072]{1,0:T(8,128)(2,1)} %copy-done.56, bf16[1024,768]{1,0:T(8,128)(2,1)} %get-tuple-element.187), kind=kOutput, calls=%fused_computation.191 | convolution fusion | flops 4831838208 | bytes 17301504 | tf_op jit(solution)/shard_map/dot_general | solution.py:199
  306.1 4.0 dynamic-slice_convert_fusion
  311.2 2.6 convert_add_fusion.1
  316.0 2.4 fusion.32
  320.1 3.5 convert_add_fusion
  324.4 6.0 %collective-permute-done.21 = bf16[192,3072]{1,0:T(8,128)(2,1)} collective-permute-done((bf16[192,3072]{1,0:T(8,128)(2,1)S(1)}, bf16[192,3072]{1,0:T(8,128)(2,1)}, u32[]{:S(2)}, u32[]{:S(2)}) %collective-permute-start.21) | collective-permute-done | bytes 1179680 | tf_op jit(solution)/shard_map/ppermute | solution.py:30
  334.1 15.1 %collective-permute-done.6 = bf16[192,3072]{1,0:T(8,128)(2,1)S(1)} collective-permute-done((bf16[192,3072]{1,0:T(8,128)(2,1)S(1)}, bf16[192,3072]{1,0:T(8,128)(2,1)S(1)}, u32[]{:S(2)}, u32[]{:S(2)}) %collective-permute-start.6) | collective-permute-done | bytes 1179680 | tf_op jit(solution)/shard_map/ppermute | solution.py:30
  351.7 16.5 %collective-permute-done.31 = bf16[768,768]{1,0:T(8,128)(2,1)S(1)} collective-permute-done((bf16[768,768]{1,0:T(8,128)(2,1)S(1)}, bf16[768,768]{1,0:T(8,128)(2,1)S(1)}, u32[]{:S(2)}, u32[]{:S(2)}) %collective-permute-start.31) | collective-permute-done | bytes 1179680 | tf_op jit(solution)/shard_map/ppermute | solution.py:30
  373.1 5.4 collective-permute-done.32
  380.8 2.6 collective-permute-start.24
  383.5 8.3 %collective-permute-done.8 = bf16[48,3072]{1,0:T(8,128)(2,1)S(1)} collective-permute-done((bf16[48,3072]{1,0:T(8,128)(2,1)S(1)}, bf16[48,3072]{1,0:T(8,128)(2,1)S(1)}, u32[]{:S(2)}, u32[]{:S(2)}) %collective-permute-start.8) | collective-permute-done | bytes 294944 | tf_op jit(solution)/shard_map/ppermute | solution.py:30
  393.6 2.4 collective-permute-done.33
  399.2 11.2 %collective-permute-done.9 = bf16[24,3072]{1,0:T(8,128)(2,1)S(1)} collective-permute-done((bf16[24,3072]{1,0:T(8,128)(2,1)S(1)}, bf16[24,3072]{1,0:T(8,128)(2,1)S(1)}, u32[]{:S(2)}, u32[]{:S(2)}) %collective-permute-start.9) | collective-permute-done | bytes 147488 | tf_op jit(solution)/shard_map/ppermute | solution.py:30
  410.6 7.8 %collective-permute-done.34 = bf16[96,768]{1,0:T(8,128)(2,1)S(1)} collective-permute-done((bf16[96,768]{1,0:T(8,128)(2,1)S(1)}, bf16[96,768]{1,0:T(8,128)(2,1)S(1)}, u32[]{:S(2)}, u32[]{:S(2)}) %collective-permute-start.34) | collective-permute-done | bytes 147488 | tf_op jit(solution)/shard_map/ppermute | solution.py:30
  418.5 6.2 %collective-permute-done.10 = bf16[24,3072]{1,0:T(8,128)(2,1)S(1)} collective-permute-done((bf16[24,3072]{1,0:T(8,128)(2,1)S(1)}, bf16[24,3072]{1,0:T(8,128)(2,1)S(1)}, u32[]{:S(2)}, u32[]{:S(2)}) %collective-permute-start.10) | collective-permute-done | bytes 147488 | tf_op jit(solution)/shard_map/ppermute | solution.py:30
  427.0 7.7 %collective-permute-done.11 = bf16[48,3072]{1,0:T(8,128)(2,1)S(1)} collective-permute-done((bf16[48,3072]{1,0:T(8,128)(2,1)S(1)}, bf16[48,3072]{1,0:T(8,128)(2,1)S(1)}, u32[]{:S(2)}, u32[]{:S(2)}) %collective-permute-start.11) | collective-permute-done | bytes 294944 | tf_op jit(solution)/shard_map/ppermute | solution.py:30
  436.3 4.8 collective-permute-done.26
  442.5 2.9 collective-permute-done.36
  448.1 20.2 %collective-permute-done.37 = bf16[384,768]{1,0:T(8,128)(2,1)S(1)} collective-permute-done((bf16[384,768]{1,0:T(8,128)(2,1)S(1)}, bf16[384,768]{1,0:T(8,128)(2,1)S(1)}, u32[]{:S(2)}, u32[]{:S(2)}) %collective-permute-start.37) | collective-permute-done | bytes 589856 | tf_op jit(solution)/shard_map/ppermute | solution.py:30
  480.5 19.1 %collective-permute-done.16 = f32[32,384]{1,0:T(8,128)S(1)} collective-permute-done((f32[32,384]{1,0:T(8,128)S(1)}, f32[32,384]{1,0:T(8,128)S(1)}, u32[]{:S(2)}, u32[]{:S(2)}) %collective-permute-start.16) | collective-permute-done | bytes 49184 | tf_op jit(solution)/shard_map/ppermute | solution.py:30
  500.1 3.8 collective-permute-done.17
  504.1 3.8 maximum_select_fusion.5
  508.1 4.2 maximum_select_fusion.4
  512.7 7.9 %add_add_fusion.4 = f32[1024,768]{1,0:T(8,128)} fusion(f32[1024,768]{1,0:T(8,128)S(1)} %copy-done.14, bf16[1024,2304]{1,0:T(8,128)(2,1)} %bitcast.172, bf16[768,2304]{1,0:T(8,128)(2,1)S(1)} %copy-done, f32[1024]{0:T(1024)S(1)} %copy-done.40), kind=kOutput, calls=%fused_computation.100 | convolution fusion | flops 3625451520 | bytes 14553088 | tf_op jit(solution)/shard_map/dot_general | solution.py:205
  530.9 4.7 fusion.33
  537.2 3.5 slice.116
  540.7 8.6 %fusion.35 = f32[3072,768]{1,0:T(8,128)} fusion(bf16[1536,768]{1,0:T(8,128)(2,1)} %collective-permute-done.39, bf16[1536,768]{1,0:T(8,128)(2,1)} %maximum_select_fusion.5, pred[]{:T(512)S(6)} %eq.147), kind=kLoop, calls=%fused_computation.81 | loop fusion | flops 23592960 | bytes 14155777 | tf_op jit(solution)/shard_map/convert_element_type | solution.py:58
  549.3 9.4 %fusion.34 = f32[768,3072]{1,0:T(8,128)} fusion(bf16[384,3072]{1,0:T(8,128)(2,1)} %collective-permute-done.29, bf16[384,3072]{1,0:T(8,128)(2,1)} %maximum_select_fusion.4, pred[]{:T(512)S(6)} %eq.147), kind=kLoop, calls=%fused_computation.79 | loop fusion | flops 23592960 | bytes 14155777 | tf_op jit(solution)/shard_map/convert_element_type | solution.py:58
  (341 shorter events, 143.3 us)
Async XLA Ops:
  16.8 36.8 %copy-start.54 = (f32[768]{0:T(1024)S(1)}, f32[768]{0:T(1024)}, u32[]{:S(2)}) copy-start(f32[768]{0:T(1024)} %param.29) | copy-start | bytes 9220
  53.5 40.6 %slice-start.2 = ((s8[4718592]{0:T(1024)(128)(4,1)}), s8[4194304]{0:T(1024)(128)(4,1)S(1)}, s32[]{:S(2)}) async-start(s8[4718592]{0:T(1024)(128)(4,1)} %bitcast.179), calls=%async_computation.2 | async-start | bytes 8388608
  57.5 36.7 %copy-start.10 = (f32[1024,768]{1,0:T(8,128)}, f32[1024,768]{1,0:T(8,128)S(1)}, u32[]{:S(2)}) copy-start(f32[1024,768]{1,0:T(8,128)S(1)} %get-tuple-element.211) | copy-start | bytes 9437188
  59.1 35.1 %slice-start.3 = ((s8[4718592]{0:T(1024)(128)(4,1)}), s8[524288]{0:T(1024)(128)(4,1)S(1)}, s32[]{:S(2)}) async-start(s8[4718592]{0:T(1024)(128)(4,1)} %bitcast.179), calls=%async_computation.3 | async-start | bytes 1048576
  59.1 35.1 %copy-start.55 = (f32[768]{0:T(1024)S(1)}, f32[768]{0:T(1024)}, u32[]{:S(2)}) copy-start(f32[768]{0:T(1024)} %param.35) | copy-start | bytes 9220
  102.2 30.1 %copy-start.1 = (s32[512]{0:T(512)S(1)}, s32[512]{0:T(512)}, u32[]{:S(2)}) copy-start(s32[512]{0:T(512)} %param.23) | copy-start | bytes 6148
  104.0 6.2 %collective-permute-start = (bf16[16,768]{1,0:T(8,128)(2,1)}, bf16[16,768]{1,0:T(8,128)(2,1)}, u32[]{:S(2)}, u32[]{:S(2)}) collective-permute-start(bf16[16,768]{1,0:T(8,128)(2,1)} %fusion.39.own_ref), channel_id=1, source_target_pairs={{0,16},{1,17},{2,18},{3,19},{4,20},{5,21},{6,22},{7,23},{8,24},{9,... | collective-permute-start | bytes 73736 | tf_op jit(solution)/shard_map/ppermute | solution.py:30
  111.6 4.4 collective-permute-start.1
  117.6 4.9 collective-permute-start.2
  124.3 6.0 %collective-permute-start.3 = (bf16[128,768]{1,0:T(8,128)(2,1)}, bf16[128,768]{1,0:T(8,128)(2,1)}, u32[]{:S(2)}, u32[]{:S(2)}) collective-permute-start(bf16[128,768]{1,0:T(8,128)(2,1)} %maximum_select_fusion.17), channel_id=1, source_target_pairs={{0,2},{1,3},{2,0},{3,1},{4,6},{5,7},{6,4},{7,5},{8,10},{9,11},{10,... | collective-permute-start | bytes 589832 | tf_op jit(solution)/shard_map/ppermute | solution.py:30
  132.3 14.7 %collective-permute-start.4 = (bf16[256,768]{1,0:T(8,128)(2,1)}, bf16[256,768]{1,0:T(8,128)(2,1)}, u32[]{:S(2)}, u32[]{:S(2)}) collective-permute-start(bf16[256,768]{1,0:T(8,128)(2,1)} %maximum_select_fusion.13), channel_id=1, source_target_pairs={{0,1},{1,0},{2,3},{3,2},{4,5},{5,4},{6,7},{7,6},{8,9},{9,8},{10,11... | collective-permute-start | bytes 1179656 | tf_op jit(solution)/shard_map/ppermute | solution.py:30
  147.0 11.8 %copy-start.25 = (f32[1024]{0:T(1024)S(1)}, f32[1024]{0:T(1024)}, u32[]{:S(2)}) copy-start(f32[1024]{0:T(1024)} %copy-done.24) | copy-start | bytes 12292
  147.0 11.8 %copy-start.9 = (f32[1024,768]{1,0:T(8,128)S(1)}, f32[1024,768]{1,0:T(8,128)}, u32[]{:S(2)}) copy-start(f32[1024,768]{1,0:T(8,128)} %copy-done.8) | copy-start | bytes 9437188
  147.0 11.8 %copy-start.29 = (f32[1024]{0:T(1024)S(1)}, f32[1024]{0:T(1024)}, u32[]{:S(2)}) copy-start(f32[1024]{0:T(1024)} %copy-done.28) | copy-start | bytes 12292
  147.0 11.8 %copy-start.38 = (f32[768]{0:T(1024)S(1)}, f32[768]{0:T(1024)}, u32[]{:S(2)}) copy-start(f32[768]{0:T(1024)} %param.36) | copy-start | bytes 9220
  164.3 18.9 %copy-start.11 = (f32[1024,768]{1,0:T(8,128)S(1)}, f32[1024,768]{1,0:T(8,128)}, u32[]{:S(2)}) copy-start(f32[1024,768]{1,0:T(8,128)} %copy-done.10) | copy-start | bytes 9437188
  164.3 18.9 %copy-start.27 = (f32[768]{0:T(1024)S(1)}, f32[768]{0:T(1024)}, u32[]{:S(2)}) copy-start(f32[768]{0:T(1024)} %param.30) | copy-start | bytes 9220
  183.1 11.2 %copy-start.18 = (bf16[1024,3072]{1,0:T(8,128)(2,1)S(1)}, bf16[1024,3072]{1,0:T(8,128)(2,1)}, u32[]{:S(2)}) copy-start(bf16[1024,3072]{1,0:T(8,128)(2,1)} %get-tuple-element.217) | copy-start | bytes 18874372
  183.1 11.2 %copy-start.31 = (f32[768]{0:T(1024)S(1)}, f32[768]{0:T(1024)}, u32[]{:S(2)}) copy-start(f32[768]{0:T(1024)} %param.31) | copy-start | bytes 9220
  194.3 8.5 %copy-start.33 = (f32[1024]{0:T(1024)S(1)}, f32[1024]{0:T(1024)}, u32[]{:S(2)}) copy-start(f32[1024]{0:T(1024)} %copy-done.32) | copy-start | bytes 12292
  284.8 7.2 %copy-start.12 = (f32[768,3072]{1,0:T(8,128)S(1)}, f32[768,3072]{1,0:T(8,128)}, u32[]{:S(2)}) copy-start(f32[768,3072]{1,0:T(8,128)} %fusion.46) | copy-start | bytes 28311556
  292.4 18.8 %collective-permute-start.20 = (bf16[384,3072]{1,0:T(8,128)(2,1)S(1)}, bf16[384,3072]{1,0:T(8,128)(2,1)}, u32[]{:S(2)}, u32[]{:S(2)}) collective-permute-start(bf16[384,3072]{1,0:T(8,128)(2,1)S(1)} %dynamic-slice_convert_fusion.1), channel_id=1, source_target_pairs={{0,1},{1,0},{2,3},{3,2},{4,5},{5,4},{6,7},{7,6},{8,9},{9,8},{10,11... | collective-permute-start | bytes 7077896 | tf_op jit(solution)/shard_map/ppermute | solution.py:30
  293.7 16.8 %slice-start = ((s8[4718592]{0:T(1024)(128)(4,1)}), s8[4194304]{0:T(1024)(128)(4,1)S(1)}, s32[]{:S(2)}) async-start(s8[4718592]{0:T(1024)(128)(4,1)} %bitcast.167), calls=%async_computation | async-start | bytes 8388608
  295.5 15.0 %slice-start.1 = ((s8[4718592]{0:T(1024)(128)(4,1)}), s8[524288]{0:T(1024)(128)(4,1)S(1)}, s32[]{:S(2)}) async-start(s8[4718592]{0:T(1024)(128)(4,1)} %bitcast.167), calls=%async_computation.1 | async-start | bytes 1048576
  295.5 20.5 %collective-permute-start.5 = (bf16[384,3072]{1,0:T(8,128)(2,1)}, bf16[384,3072]{1,0:T(8,128)(2,1)}, u32[]{:S(2)}, u32[]{:S(2)}) collective-permute-start(bf16[384,3072]{1,0:T(8,128)(2,1)} %fusion.30), channel_id=1, source_target_pairs={{0,1},{1,0},{2,3},{3,2},{4,5},{5,4},{6,7},{7,6},{8,9},{9,8},{10,11... | collective-permute-start | bytes 7077896 | tf_op jit(solution)/shard_map/ppermute | solution.py:30
  310.1 10.0 %collective-permute-start.30 = (bf16[1536,768]{1,0:T(8,128)(2,1)}, bf16[1536,768]{1,0:T(8,128)(2,1)}, u32[]{:S(2)}, u32[]{:S(2)}) collective-permute-start(bf16[1536,768]{1,0:T(8,128)(2,1)} %dynamic-slice_convert_fusion), channel_id=1, source_target_pairs={{0,1},{1,0},{2,3},{3,2},{4,5},{5,4},{6,7},{7,6},{8,9},{9,8},{10,11... | collective-permute-start | bytes 7077896 | tf_op jit(solution)/shard_map/ppermute | solution.py:30
  314.0 16.4 %collective-permute-start.21 = (bf16[192,3072]{1,0:T(8,128)(2,1)S(1)}, bf16[192,3072]{1,0:T(8,128)(2,1)}, u32[]{:S(2)}, u32[]{:S(2)}) collective-permute-start(bf16[192,3072]{1,0:T(8,128)(2,1)S(1)} %dynamic-slice_convert_fusion.3), channel_id=1, source_target_pairs={{0,2},{1,5},{2,0},{3,7},{4,6},{5,1},{6,4},{7,3},{8,10},{9,13},{10,... | collective-permute-start | bytes 3538952 | tf_op jit(solution)/shard_map/ppermute | solution.py:30
  318.6 30.6 %collective-permute-start.6 = (bf16[192,3072]{1,0:T(8,128)(2,1)S(1)}, bf16[192,3072]{1,0:T(8,128)(2,1)S(1)}, u32[]{:S(2)}, u32[]{:S(2)}) collective-permute-start(bf16[192,3072]{1,0:T(8,128)(2,1)S(1)} %dynamic-slice_convert_fusion.4), channel_id=1, source_target_pairs={{0,2},{1,5},{2,0},{3,7},{4,6},{5,1},{6,4},{7,3},{8,10},{9,13},{10,... | collective-permute-start | bytes 3538952 | tf_op jit(solution)/shard_map/ppermute | solution.py:30
  323.7 44.5 %collective-permute-start.31 = (bf16[768,768]{1,0:T(8,128)(2,1)S(1)}, bf16[768,768]{1,0:T(8,128)(2,1)S(1)}, u32[]{:S(2)}, u32[]{:S(2)}) collective-permute-start(bf16[768,768]{1,0:T(8,128)(2,1)S(1)} %dynamic-slice_convert_fusion.2), channel_id=1, source_target_pairs={{0,2},{1,5},{2,0},{3,7},{4,6},{5,1},{6,4},{7,3},{8,10},{9,13},{10,... | collective-permute-start | bytes 3538952 | tf_op jit(solution)/shard_map/ppermute | solution.py:30
  332.1 38.5 %collective-permute-start.22 = (bf16[96,3072]{1,0:T(8,128)(2,1)S(1)}, bf16[96,3072]{1,0:T(8,128)(2,1)S(1)}, u32[]{:S(2)}, u32[]{:S(2)}) collective-permute-start(bf16[96,3072]{1,0:T(8,128)(2,1)S(1)} %dynamic-slice_convert_fusion.6), channel_id=1, source_target_pairs={{0,4},{1,3},{2,6},{3,1},{4,0},{5,7},{6,2},{7,5},{8,12},{9,11},{10,... | collective-permute-start | bytes 1769480 | tf_op jit(solution)/shard_map/ppermute | solution.py:30
  349.7 22.6 %collective-permute-start.7 = (bf16[96,3072]{1,0:T(8,128)(2,1)S(1)}, bf16[96,3072]{1,0:T(8,128)(2,1)S(1)}, u32[]{:S(2)}, u32[]{:S(2)}) collective-permute-start(bf16[96,3072]{1,0:T(8,128)(2,1)S(1)} %dynamic-slice_convert_fusion.7), channel_id=1, source_target_pairs={{0,4},{1,3},{2,6},{3,1},{4,0},{5,7},{6,2},{7,5},{8,12},{9,11},{10,... | collective-permute-start | bytes 1769480 | tf_op jit(solution)/shard_map/ppermute | solution.py:30
  368.5 9.9 %collective-permute-start.32 = (bf16[384,768]{1,0:T(8,128)(2,1)S(1)}, bf16[384,768]{1,0:T(8,128)(2,1)S(1)}, u32[]{:S(2)}, u32[]{:S(2)}) collective-permute-start(bf16[384,768]{1,0:T(8,128)(2,1)S(1)} %dynamic-slice_convert_fusion.5), channel_id=1, source_target_pairs={{0,4},{1,3},{2,6},{3,1},{4,0},{5,7},{6,2},{7,5},{8,12},{9,11},{10,... | collective-permute-start | bytes 1769480 | tf_op jit(solution)/shard_map/ppermute | solution.py:30
  370.7 10.0 %collective-permute-start.23 = (bf16[48,3072]{1,0:T(8,128)(2,1)S(1)}, bf16[48,3072]{1,0:T(8,128)(2,1)S(1)}, u32[]{:S(2)}, u32[]{:S(2)}) collective-permute-start(bf16[48,3072]{1,0:T(8,128)(2,1)S(1)} %dynamic-slice_convert_fusion.9), channel_id=1, source_target_pairs={{0,8},{1,9},{2,10},{3,11},{4,12},{5,13},{6,14},{7,15},{8,0},{9,1},... | collective-permute-start | bytes 884744 | tf_op jit(solution)/shard_map/ppermute | solution.py:30
  372.4 19.4 %collective-permute-start.8 = (bf16[48,3072]{1,0:T(8,128)(2,1)S(1)}, bf16[48,3072]{1,0:T(8,128)(2,1)S(1)}, u32[]{:S(2)}, u32[]{:S(2)}) collective-permute-start(bf16[48,3072]{1,0:T(8,128)(2,1)S(1)} %dynamic-slice_convert_fusion.10), channel_id=1, source_target_pairs={{0,8},{1,9},{2,10},{3,11},{4,12},{5,13},{6,14},{7,15},{8,0},{9,1},... | collective-permute-start | bytes 884744 | tf_op jit(solution)/shard_map/ppermute | solution.py:30
  378.6 17.4 %collective-permute-start.33 = (bf16[192,768]{1,0:T(8,128)(2,1)S(1)}, bf16[192,768]{1,0:T(8,128)(2,1)S(1)}, u32[]{:S(2)}, u32[]{:S(2)}) collective-permute-start(bf16[192,768]{1,0:T(8,128)(2,1)S(1)} %dynamic-slice_convert_fusion.8), channel_id=1, source_target_pairs={{0,8},{1,9},{2,10},{3,11},{4,12},{5,13},{6,14},{7,15},{8,0},{9,1},... | collective-permute-start | bytes 884744 | tf_op jit(solution)/shard_map/ppermute | solution.py:30
  380.8 17.1 %collective-permute-start.24 = (bf16[24,3072]{1,0:T(8,128)(2,1)S(1)}, bf16[24,3072]{1,0:T(8,128)(2,1)S(1)}, u32[]{:S(2)}, u32[]{:S(2)}) collective-permute-start(bf16[24,3072]{1,0:T(8,128)(2,1)S(1)} %dynamic-slice_convert_fusion.12), channel_id=1, source_target_pairs={{0,16},{1,17},{2,18},{3,19},{4,20},{5,21},{6,22},{7,23},{8,24},{9,... | collective-permute-start | bytes 442376 | tf_op jit(solution)/shard_map/ppermute | solution.py:30
  391.9 18.6 %collective-permute-start.9 = (bf16[24,3072]{1,0:T(8,128)(2,1)S(1)}, bf16[24,3072]{1,0:T(8,128)(2,1)S(1)}, u32[]{:S(2)}, u32[]{:S(2)}) collective-permute-start(bf16[24,3072]{1,0:T(8,128)(2,1)S(1)} %dynamic-slice_convert_fusion.13), channel_id=1, source_target_pairs={{0,16},{1,17},{2,18},{3,19},{4,20},{5,21},{6,22},{7,23},{8,24},{9,... | collective-permute-start | bytes 442376 | tf_op jit(solution)/shard_map/ppermute | solution.py:30
  396.1 22.2 %collective-permute-start.34 = (bf16[96,768]{1,0:T(8,128)(2,1)S(1)}, bf16[96,768]{1,0:T(8,128)(2,1)S(1)}, u32[]{:S(2)}, u32[]{:S(2)}) collective-permute-start(bf16[96,768]{1,0:T(8,128)(2,1)S(1)} %dynamic-slice_convert_fusion.11), channel_id=1, source_target_pairs={{0,16},{1,17},{2,18},{3,19},{4,20},{5,21},{6,22},{7,23},{8,24},{9,... | collective-permute-start | bytes 442376 | tf_op jit(solution)/shard_map/ppermute | solution.py:30
  398.0 26.9 %collective-permute-start.25 = (bf16[24,3072]{1,0:T(8,128)(2,1)S(1)}, bf16[24,3072]{1,0:T(8,128)(2,1)S(1)}, u32[]{:S(2)}, u32[]{:S(2)}) collective-permute-start(bf16[24,3072]{1,0:T(8,128)(2,1)S(1)} %add_convert_fusion.5), channel_id=1, source_target_pairs={{0,16},{1,17},{2,18},{3,19},{4,20},{5,21},{6,22},{7,23},{8,24},{9,... | collective-permute-start | bytes 442376 | tf_op jit(solution)/shard_map/ppermute | solution.py:30
  410.5 14.2 %collective-permute-start.10 = (bf16[24,3072]{1,0:T(8,128)(2,1)S(1)}, bf16[24,3072]{1,0:T(8,128)(2,1)S(1)}, u32[]{:S(2)}, u32[]{:S(2)}) collective-permute-start(bf16[24,3072]{1,0:T(8,128)(2,1)S(1)} %add_convert_fusion.6), channel_id=1, source_target_pairs={{0,16},{1,17},{2,18},{3,19},{4,20},{5,21},{6,22},{7,23},{8,24},{9,... | collective-permute-start | bytes 442376 | tf_op jit(solution)/shard_map/ppermute | solution.py:30
  418.4 17.7 %collective-permute-start.35 = (bf16[96,768]{1,0:T(8,128)(2,1)S(1)}, bf16[96,768]{1,0:T(8,128)(2,1)S(1)}, u32[]{:S(2)}, u32[]{:S(2)}) collective-permute-start(bf16[96,768]{1,0:T(8,128)(2,1)S(1)} %add_convert_fusion.4), channel_id=1, source_target_pairs={{0,16},{1,17},{2,18},{3,19},{4,20},{5,21},{6,22},{7,23},{8,24},{9,... | collective-permute-start | bytes 442376 | tf_op jit(solution)/shard_map/ppermute | solution.py:30
  424.8 10.0 %collective-permute-start.11 = (bf16[48,3072]{1,0:T(8,128)(2,1)S(1)}, bf16[48,3072]{1,0:T(8,128)(2,1)S(1)}, u32[]{:S(2)}, u32[]{:S(2)}) collective-permute-start(bf16[48,3072]{1,0:T(8,128)(2,1)S(1)} %maximum_select_fusion.14), channel_id=1, source_target_pairs={{0,8},{1,9},{2,10},{3,11},{4,12},{5,13},{6,14},{7,15},{8,0},{9,1},... | collective-permute-start | bytes 884744 | tf_op jit(solution)/shard_map/ppermute | solution.py:30
  424.9 23.1 %copy-start.43 = (f32[768]{0:T(1024)S(1)}, f32[768]{0:T(1024)}, u32[]{:S(2)}) copy-start(f32[768]{0:T(1024)} %get-tuple-element.188) | copy-start | bytes 9220
  424.9 23.1 %copy-start.49 = (f32[768]{0:T(1024)S(1)}, f32[768]{0:T(1024)}, u32[]{:S(2)}) copy-start(f32[768]{0:T(1024)} %get-tuple-element.161) | copy-start | bytes 9220
  425.0 23.1 %copy-start.48 = (f32[768]{0:T(1024)S(1)}, f32[768]{0:T(1024)}, u32[]{:S(2)}) copy-start(f32[768]{0:T(1024)} %get-tuple-element.163) | copy-start | bytes 9220
  425.0 23.1 %copy-start.45 = (f32[3072]{0:T(1024)S(1)}, f32[3072]{0:T(1024)}, u32[]{:S(2)}) copy-start(f32[3072]{0:T(1024)} %get-tuple-element.216) | copy-start | bytes 36868
  425.0 16.1 %collective-permute-start.26 = (bf16[48,3072]{1,0:T(8,128)(2,1)S(1)}, bf16[48,3072]{1,0:T(8,128)(2,1)S(1)}, u32[]{:S(2)}, u32[]{:S(2)}) collective-permute-start(bf16[48,3072]{1,0:T(8,128)(2,1)S(1)} %maximum_select_fusion.15), channel_id=1, source_target_pairs={{0,8},{1,9},{2,10},{3,11},{4,12},{5,13},{6,14},{7,15},{8,0},{9,1},... | collective-permute-start | bytes 884744 | tf_op jit(solution)/shard_map/ppermute | solution.py:30
  434.9 12.1 %collective-permute-start.12 = (bf16[96,3072]{1,0:T(8,128)(2,1)S(1)}, bf16[96,3072]{1,0:T(8,128)(2,1)S(1)}, u32[]{:S(2)}, u32[]{:S(2)}) collective-permute-start(bf16[96,3072]{1,0:T(8,128)(2,1)S(1)} %maximum_select_fusion.10), channel_id=1, source_target_pairs={{0,4},{1,3},{2,6},{3,1},{4,0},{5,7},{6,2},{7,5},{8,12},{9,11},{10,... | collective-permute-start | bytes 1769480 | tf_op jit(solution)/shard_map/ppermute | solution.py:30
  436.2 9.1 %collective-permute-start.36 = (bf16[192,768]{1,0:T(8,128)(2,1)S(1)}, bf16[192,768]{1,0:T(8,128)(2,1)S(1)}, u32[]{:S(2)}, u32[]{:S(2)}) collective-permute-start(bf16[192,768]{1,0:T(8,128)(2,1)S(1)} %maximum_select_fusion.16), channel_id=1, source_target_pairs={{0,8},{1,9},{2,10},{3,11},{4,12},{5,13},{6,14},{7,15},{8,0},{9,1},... | collective-permute-start | bytes 884744 | tf_op jit(solution)/shard_map/ppermute | solution.py:30
  441.2 28.5 %collective-permute-start.27 = (bf16[96,3072]{1,0:T(8,128)(2,1)S(1)}, bf16[96,3072]{1,0:T(8,128)(2,1)S(1)}, u32[]{:S(2)}, u32[]{:S(2)}) collective-permute-start(bf16[96,3072]{1,0:T(8,128)(2,1)S(1)} %maximum_select_fusion.11), channel_id=1, source_target_pairs={{0,4},{1,3},{2,6},{3,1},{4,0},{5,7},{6,2},{7,5},{8,12},{9,11},{10,... | collective-permute-start | bytes 1769480 | tf_op jit(solution)/shard_map/ppermute | solution.py:30
  445.5 27.4 %copy-start.42 = (f32[768]{0:T(1024)S(1)}, f32[768]{0:T(1024)}, u32[]{:S(2)}) copy-start(f32[768]{0:T(1024)} %get-tuple-element.186) | copy-start | bytes 9220
  445.6 27.4 %copy-start.44 = (f32[768]{0:T(1024)S(1)}, f32[768]{0:T(1024)}, u32[]{:S(2)}) copy-start(f32[768]{0:T(1024)} %get-tuple-element.159) | copy-start | bytes 9220
  445.6 22.7 %collective-permute-start.37 = (bf16[384,768]{1,0:T(8,128)(2,1)S(1)}, bf16[384,768]{1,0:T(8,128)(2,1)S(1)}, u32[]{:S(2)}, u32[]{:S(2)}) collective-permute-start(bf16[384,768]{1,0:T(8,128)(2,1)S(1)} %maximum_select_fusion.12), channel_id=1, source_target_pairs={{0,4},{1,3},{2,6},{3,1},{4,0},{5,7},{6,2},{7,5},{8,12},{9,11},{10,... | collective-permute-start | bytes 1769480 | tf_op jit(solution)/shard_map/ppermute | solution.py:30
  447.2 25.8 %collective-permute-start.13 = (bf16[192,3072]{1,0:T(8,128)(2,1)S(1)}, bf16[192,3072]{1,0:T(8,128)(2,1)S(1)}, u32[]{:S(2)}, u32[]{:S(2)}) collective-permute-start(bf16[192,3072]{1,0:T(8,128)(2,1)S(1)} %maximum_select_fusion.6), channel_id=1, source_target_pairs={{0,2},{1,5},{2,0},{3,7},{4,6},{5,1},{6,4},{7,3},{8,10},{9,13},{10,... | collective-permute-start | bytes 3538952 | tf_op jit(solution)/shard_map/ppermute | solution.py:30
  469.7 34.3 %collective-permute-start.38 = (bf16[768,768]{1,0:T(8,128)(2,1)}, bf16[768,768]{1,0:T(8,128)(2,1)}, u32[]{:S(2)}, u32[]{:S(2)}) collective-permute-start(bf16[768,768]{1,0:T(8,128)(2,1)} %maximum_select_fusion.8), channel_id=1, source_target_pairs={{0,2},{1,5},{2,0},{3,7},{4,6},{5,1},{6,4},{7,3},{8,10},{9,13},{10,... | collective-permute-start | bytes 3538952 | tf_op jit(solution)/shard_map/ppermute | solution.py:30
  471.0 37.1 %collective-permute-start.28 = (bf16[192,3072]{1,0:T(8,128)(2,1)}, bf16[192,3072]{1,0:T(8,128)(2,1)}, u32[]{:S(2)}, u32[]{:S(2)}) collective-permute-start(bf16[192,3072]{1,0:T(8,128)(2,1)} %maximum_select_fusion.7), channel_id=1, source_target_pairs={{0,2},{1,5},{2,0},{3,7},{4,6},{5,1},{6,4},{7,3},{8,10},{9,13},{10,... | collective-permute-start | bytes 3538952 | tf_op jit(solution)/shard_map/ppermute | solution.py:30
  474.9 56.0 %collective-permute-start.14 = (bf16[384,3072]{1,0:T(8,128)(2,1)}, bf16[384,3072]{1,0:T(8,128)(2,1)}, u32[]{:S(2)}, u32[]{:S(2)}) collective-permute-start(bf16[384,3072]{1,0:T(8,128)(2,1)} %maximum_select_fusion.3), channel_id=1, source_target_pairs={{0,1},{1,0},{2,3},{3,2},{4,5},{5,4},{6,7},{7,6},{8,9},{9,8},{10,11... | collective-permute-start | bytes 7077896 | tf_op jit(solution)/shard_map/ppermute | solution.py:30
  477.0 2.8 collective-permute-start.15
  480.5 19.2 %collective-permute-start.16 = (f32[32,384]{1,0:T(8,128)S(1)}, f32[32,384]{1,0:T(8,128)S(1)}, u32[]{:S(2)}, u32[]{:S(2)}) collective-permute-start(f32[32,384]{1,0:T(8,128)S(1)} %add.468), channel_id=1, source_target_pairs={{0,2},{1,5},{2,0},{3,7},{4,6},{5,1},{6,4},{7,3},{8,10},{9,13},{10,... | collective-permute-start | bytes 147464 | tf_op jit(solution)/shard_map/ppermute | solution.py:30
  499.7 4.2 collective-permute-start.17
  503.8 4.2 collective-permute-start.18
  507.9 32.8 %collective-permute-start.39 = (bf16[1536,768]{1,0:T(8,128)(2,1)}, bf16[1536,768]{1,0:T(8,128)(2,1)}, u32[]{:S(2)}, u32[]{:S(2)}) collective-permute-start(bf16[1536,768]{1,0:T(8,128)(2,1)} %maximum_select_fusion.5), channel_id=1, source_target_pairs={{0,1},{1,0},{2,3},{3,2},{4,5},{5,4},{6,7},{7,6},{8,9},{9,8},{10,11... | collective-permute-start | bytes 7077896 | tf_op jit(solution)/shard_map/ppermute | solution.py:30
  508.0 12.6 %collective-permute-start.19 = (f32[32,384]{1,0:T(8,128)S(1)}, f32[32,384]{1,0:T(8,128)S(1)}, u32[]{:S(2)}, u32[]{:S(2)}) collective-permute-start(f32[32,384]{1,0:T(8,128)S(1)} %add.471), channel_id=1, source_target_pairs={{0,16},{1,17},{2,18},{3,19},{4,20},{5,21},{6,22},{7,23},{8,24},{9,... | collective-permute-start | bytes 147464 | tf_op jit(solution)/shard_map/ppermute | solution.py:30
  512.3 37.0 %collective-permute-start.29 = (bf16[384,3072]{1,0:T(8,128)(2,1)}, bf16[384,3072]{1,0:T(8,128)(2,1)}, u32[]{:S(2)}, u32[]{:S(2)}) collective-permute-start(bf16[384,3072]{1,0:T(8,128)(2,1)} %maximum_select_fusion.4), channel_id=1, source_target_pairs={{0,1},{1,0},{2,3},{3,2},{4,5},{5,4},{6,7},{7,6},{8,9},{9,8},{10,11... | collective-permute-start | bytes 7077896 | tf_op jit(solution)/shard_map/ppermute | solution.py:30
  (48 other events, 146.8 us)
